TPU v7x, 32 devices: a whole 2x2x4 slice. The times are simulated.
32 devices in a mesh: img: 4 (over y, x), row: 8 (over z, core).
Axes of the slice: x: 2, y: 2, z: 4, core: 2. Of those that a mesh axis runs over, the one named last changes fastest.
Arguments:
- kspace: float32 [2, 4, 16, 2, 320, 320], P(None, 'img', None, None, 'row'), may hold values from -6 to 6
- coil_maps: float32 [2, 4, 16, 2, 320, 320], P(None, 'img', None, None, 'row'), may hold values from -1.5 to 1.5
- target: float32 [2, 4, 2, 320, 320], P(None, 'img', None, 'row'), may hold values from -6 to 6
- row_mask: int32 [2, 4, 320], P(None, 'img'), may hold values from 0 to 1, as said below
- foreground: int32 [2, 4, 320, 320], P(None, 'img', 'row'), may hold values from 0 to 1
- anatomy: int32 [2, 4], P(None, 'img'), may hold values from 0 to 1
- first_weight: float32 [9, 64, 2], replicated, may hold values from -1.5 to 1.5
- middle_weight: float32 [3, 9, 64, 64], replicated, may hold values from -0.25 to 0.25
- last_weight: float32 [9, 2, 64], replicated, may hold values from -0.25 to 0.25
- norm_gains: float32 [4, 64], replicated, may hold values from 0.5 to 1.5
- norm_shifts: float32 [4, 64], replicated, may hold values from -1.5 to 1.5
- extra_params: float32 [3], replicated, may hold values from -1.5 to 1.5
- first_mean: float32 [9, 64, 2], replicated, may hold values from -0.0048828125 to 0.0048828125
- first_square: float32 [9, 64, 2], replicated, may hold values from 1.0986328e-08 to 4.3945313e-08
- middle_mean: float32 [3, 9, 64, 64], replicated, may hold values from -0.0048828125 to 0.0048828125
- middle_square: float32 [3, 9, 64, 64], replicated, may hold values from 1.0986328e-08 to 4.3945313e-08
- last_mean: float32 [9, 2, 64], replicated, may hold values from -0.0048828125 to 0.0048828125
- last_square: float32 [9, 2, 64], replicated, may hold values from 1.0986328e-08 to 4.3945313e-08
- gains_mean: float32 [4, 64], replicated, may hold values from -0.0048828125 to 0.0048828125
- gains_square: float32 [4, 64], replicated, may hold values from 1.0986328e-08 to 4.3945313e-08
- shifts_mean: float32 [4, 64], replicated, may hold values from -0.0048828125 to 0.0048828125
- shifts_square: float32 [4, 64], replicated, may hold values from 1.0986328e-08 to 4.3945313e-08
- extra_mean: float32 [3], replicated, may hold values from -0.046875 to 0.046875
- extra_square: float32 [3], replicated, may hold values from 1.0986328e-06 to 4.394531e-06
Outputs:
- first_updated: float32 [9, 64, 2], replicated
- first_average: float32 [9, 64, 2], replicated
- first_energy: float32 [9, 64, 2], replicated
- first_copy: bfloat16 [9, 64, 2], replicated
- middle_updated: float32 [3, 9, 64, 64], replicated
- middle_average: float32 [3, 9, 64, 64], replicated
- middle_energy: float32 [3, 9, 64, 64], replicated
- middle_copy: bfloat16 [3, 9, 64, 64], replicated
- last_updated: float32 [9, 2, 64], replicated
- last_average: float32 [9, 2, 64], replicated
- last_energy: float32 [9, 2, 64], replicated
- last_copy: bfloat16 [9, 2, 64], replicated
- gains_updated: float32 [4, 64], replicated
- gains_average: float32 [4, 64], replicated
- gains_energy: float32 [4, 64], replicated
- shifts_updated: float32 [4, 64], replicated
- shifts_average: float32 [4, 64], replicated
- shifts_energy: float32 [4, 64], replicated
- extra_updated: float32 [3], replicated
- extra_average: float32 [3], replicated
- extra_energy: float32 [3], replicated
- loss_total: float32 [], replicated
- pixel_count: int32 [], replicated
Inputs may be any that keep to these rules, and one draw needn't show every extreme that they name: `row_mask`: 1 on every row with |row - 160| < 20.
All inputs are finite; a program needn't handle non-finite values.
Results may differ from a plain program's by a relative error of at most 0.004.
The roundings to bfloat16 on the way count: a program that leaves them out, or rounds other values in their place, can miss the bound.
Values may be sent and summed in bfloat16 or wider, within the bound.
A program may use at most 320 MiB of HBM per device.

v0:
```python
import jax
import jax.numpy as jnp
from jax import lax
from jax.sharding import PartitionSpec as P

COILS = 16
BRAIN_COILS = 12
UNROLLS = 1
CG_STEPS = 2
STEP = 10


PRECISE = lax.Precision.HIGHEST
EPS_NORM = 1e-05
BETA_ONE = 0.9
BETA_TWO = 0.999
ADAM_EPS = 1e-08
DECAY_RATE = 0.01
LEARN_RATES = (0.3, 0.05, 0.05, 0.4, 0.4, 0.4)


def with_halo(cells, sides, width):
    for axis, dim in sides:
        count = lax.axis_size(axis)
        ends = count - 1
        head = lax.slice_in_dim(cells, 0, width, axis=dim)
        tail = lax.slice_in_dim(cells, cells.shape[dim] - width, cells.shape[dim], axis=dim)
        cells = jnp.concatenate(
            [
                lax.ppermute(tail, axis, [(i, (i + 1) % count) for i in range(ends)]),
                cells,
                lax.ppermute(head, axis, [((i + 1) % count, i) for i in range(ends)]),
            ],
            axis=dim,
        )
    return cells


def dft_table(length, direction):
    index = jnp.arange(length, dtype=jnp.int32)
    phase = (index[:, None] * index[None, :] % length).astype(jnp.float32) * (2.0 * jnp.pi / length)
    factor = 1.0 / jnp.sqrt(jnp.float32(length))
    cosine = jnp.cos(phase) * factor
    sine = jnp.sin(phase) * factor * direction
    return jnp.stack([jnp.stack([cosine, -sine], 1), jnp.stack([sine, cosine], 1)], 0)


def along_width(field, table):
    return jnp.einsum("bcprw,pwqk->bcqrk", field, table, precision=PRECISE)


def along_height(field, table):
    return jnp.einsum("bcprw,prqk->bcqkw", field, table, precision=PRECISE)


def expand(image, maps):
    real_part, imag_part = (image[:, None, 0], image[:, None, 1])
    maps_re, maps_im = (maps[:, :, 0], maps[:, :, 1])
    return jnp.stack(
        [maps_re * real_part - maps_im * imag_part, maps_re * imag_part + maps_im * real_part], 2
    )


def combine(field, maps):
    field_re, field_im = (field[:, :, 0], field[:, :, 1])
    maps_re, maps_im = (maps[:, :, 0], maps[:, :, 1])
    return jnp.stack(
        [
            jnp.sum(maps_re * field_re + maps_im * field_im, 1),
            jnp.sum(maps_re * field_im - maps_im * field_re, 1),
        ],
        1,
    )


def to_columns(field):
    return lax.all_to_all(
        field.astype(jnp.bfloat16), "row", split_axis=4, concat_axis=3, tiled=True
    ).astype(field.dtype)


def to_rows(field):
    return lax.all_to_all(
        field.astype(jnp.bfloat16), "row", split_axis=3, concat_axis=4, tiled=True
    ).astype(field.dtype)


def make_normal(maps, mask_rows, forward, inverse, measured):
    zero_filled = combine(to_rows(along_height(measured * mask_rows, inverse)), maps)

    def normal(image):
        spectrum = to_columns(along_width(expand(image, maps), forward))
        spectrum = along_height(spectrum, forward) * mask_rows
        spectrum = to_rows(along_height(spectrum, inverse))
        return combine(along_width(spectrum, inverse), maps)

    return (normal, zero_filled)


def inner(left, right):
    return jnp.sum(left * right, axis=(1, 2, 3))


def per_image(values):
    return values[:, None, None, None]


def row_sums(values):
    return lax.psum(values, "row")


def solve(rhs, penalty, normal):
    state = jnp.zeros_like(rhs)
    residue = rhs
    search = rhs
    norm_now = row_sums(inner(residue, residue))
    kept = []
    for iterate in range(CG_STEPS):
        mapped = normal(search) + penalty * search
        curvature = row_sums(inner(search, mapped))
        stepsize = norm_now / curvature
        state = state + per_image(stepsize) * search
        residue = residue - per_image(stepsize) * mapped
        norm_next = row_sums(inner(residue, residue))
        kept.append((search, mapped, residue, norm_now, norm_next, curvature))
        search = residue + per_image(norm_next / norm_now) * search
        norm_now = norm_next
    return (state, kept)


def solve_backward(state_grad, kept, rhs, denoised, penalty, normal):
    search_grad = jnp.zeros_like(rhs)
    residue_grad = jnp.zeros_like(rhs)
    norm_grad = jnp.zeros(rhs.shape[0], jnp.float32)
    penalty_part = jnp.float32(0.0)
    for iterate in reversed(range(CG_STEPS)):
        search, mapped, residue, norm_now, norm_next, curvature = kept[iterate]
        factor_grad, along_search, joint_mapped, residue_mapped = lax.psum(
            (
                inner(search_grad, search),
                inner(state_grad, search),
                inner(residue_grad + search_grad, mapped),
                inner(residue, mapped),
            ),
            "row",
        )
        stepsize = norm_now / curvature
        factor = norm_next / norm_now
        norm_total = norm_grad + factor_grad / norm_now
        residue_full = residue_grad + search_grad + per_image(2.0 * norm_total) * residue
        stepsize_grad = along_search - (joint_mapped + 2.0 * norm_total * residue_mapped)
        curvature_grad = -stepsize_grad * norm_now / (curvature * curvature)
        mapped_grad = -per_image(stepsize) * residue_full + per_image(curvature_grad) * search
        penalty_part = penalty_part + jnp.sum(mapped_grad * search)
        search_grad = (
            per_image(factor) * search_grad
            + per_image(stepsize) * state_grad
            + per_image(curvature_grad) * mapped
            + normal(mapped_grad)
            + penalty * mapped_grad
        )
        residue_grad = residue_full
        norm_grad = -factor_grad * norm_next / (norm_now * norm_now) + stepsize_grad / curvature
    rhs_grad = residue_grad + search_grad + per_image(2.0 * norm_grad) * rhs
    penalty_part = penalty_part + jnp.sum(rhs_grad * denoised)
    return (penalty * rhs_grad, penalty_part)


def conv_forward(activation, weight):
    height, breadth = (activation.shape[2], activation.shape[3])
    padded = with_halo(activation, (("row", 2),), 1)
    padded = jnp.pad(padded, ((0, 0), (0, 0), (0, 0), (1, 1)))
    summed = jnp.zeros((activation.shape[0], weight.shape[1], height, breadth), jnp.float32)
    for tap_index in range(9):
        window = padded[
            :, :, tap_index // 3 : tap_index // 3 + height, tap_index % 3 : tap_index % 3 + breadth
        ]
        summed = summed + jnp.einsum(
            "oi,birw->borw", weight[tap_index], window, preferred_element_type=jnp.float32
        )
    return (summed, padded)


def conv_backward(upstream, padded, weight, need_input):
    height, breadth = (upstream.shape[2], upstream.shape[3])
    weight_grad = jnp.stack(
        [
            jnp.einsum(
                "borw,birw->oi",
                upstream,
                padded[
                    :,
                    :,
                    tap_index // 3 : tap_index // 3 + height,
                    tap_index % 3 : tap_index % 3 + breadth,
                ],
                preferred_element_type=jnp.float32,
            )
            for tap_index in range(9)
        ]
    )
    if not need_input:
        return (weight_grad, None)
    widened = with_halo(upstream, (("row", 2),), 1)
    widened = jnp.pad(widened, ((0, 0), (0, 0), (0, 0), (1, 1)))
    summed = jnp.zeros((upstream.shape[0], weight.shape[2], height, breadth), jnp.float32)
    for tap_index in range(9):
        start_r = 2 - tap_index // 3
        start_c = 2 - tap_index % 3
        window = widened[:, :, start_r : start_r + height, start_c : start_c + breadth]
        summed = summed + jnp.einsum(
            "oi,borw->birw", weight[tap_index], window, preferred_element_type=jnp.float32
        )
    return (weight_grad, summed)


def norm_sums(values):
    return lax.psum(values, ("img", "row"))


def channel(values):
    return values[None, :, None, None]


def cnn_forward(image, weights, gains, shifts, offset, pixels):
    activation = image.astype(jnp.bfloat16)
    kept = []
    for layer_index in range(4):
        linear, padded = conv_forward(activation, weights[layer_index])
        average = norm_sums(jnp.sum(linear, axis=(0, 2, 3))) / pixels
        centred = linear - channel(average)
        spread = norm_sums(jnp.sum(centred * centred, axis=(0, 2, 3))) / pixels
        inv_std = lax.rsqrt(spread + EPS_NORM)
        normed = centred * channel(inv_std)
        shaped = channel(gains[layer_index]) * normed + channel(shifts[layer_index])
        activation = jax.nn.silu(shaped).astype(jnp.bfloat16)
        kept.append((padded, normed, shaped, inv_std))
    result, padded = conv_forward(activation, weights[4])
    kept.append(padded)
    return (image + result + channel(offset), kept)


def cnn_backward(denoised_grad, kept, weights, gains, pixels, need_input):
    offset_grad = jnp.sum(denoised_grad, axis=(0, 2, 3))
    weight_grads = [None] * 5
    gain_grads = [None] * 4
    shift_grads = [None] * 4
    weight_grads[4], upstream = conv_backward(
        denoised_grad.astype(jnp.bfloat16), kept[4], weights[4], True
    )
    for layer_index in (3, 2, 1, 0):
        padded, normed, shaped, inv_std = kept[layer_index]
        sigmoid_val = jax.nn.sigmoid(shaped)
        shaped_grad = upstream * sigmoid_val * (1.0 + shaped * (1.0 - sigmoid_val))
        shift_local = jnp.sum(shaped_grad, axis=(0, 2, 3))
        gain_local = jnp.sum(shaped_grad * normed, axis=(0, 2, 3))
        shift_total, gain_total = lax.psum((shift_local, gain_local), ("img", "row"))
        gain_vec = gains[layer_index]
        linear_grad = channel(inv_std) * (
            shaped_grad * channel(gain_vec)
            - channel(gain_vec * shift_total / pixels)
            - normed * channel(gain_vec * gain_total / pixels)
        )
        shift_grads[layer_index] = shift_local
        gain_grads[layer_index] = gain_local
        weight_grads[layer_index], upstream = conv_backward(
            linear_grad.astype(jnp.bfloat16),
            padded,
            weights[layer_index],
            layer_index > 0 or need_input,
        )
    image_grad = None
    return (image_grad, weight_grads, jnp.stack(gain_grads), jnp.stack(shift_grads), offset_grad)


def adamw(weight, gradient, moment_one, moment_two, rate):
    first_new = BETA_ONE * moment_one + (1.0 - BETA_ONE) * gradient
    second_new = BETA_TWO * moment_two + (1.0 - BETA_TWO) * gradient * gradient
    corrected = first_new / (1.0 - BETA_ONE**STEP)
    divisor = jnp.sqrt(second_new / (1.0 - BETA_TWO**STEP)) + ADAM_EPS
    updated = weight - rate * (corrected / divisor + DECAY_RATE * weight)
    return (updated, first_new, second_new)


def local(
    kspace,
    coil_maps,
    target,
    row_mask,
    foreground,
    anatomy,
    first_weight,
    middle_weight,
    last_weight,
    norm_gains,
    norm_shifts,
    extra_params,
    first_mean,
    first_square,
    middle_mean,
    middle_square,
    last_mean,
    last_square,
    gains_mean,
    gains_square,
    shifts_mean,
    shifts_square,
    extra_mean,
    extra_square,
):
    length = kspace.shape[-1]
    forward = dft_table(length, 1.0)
    inverse = dft_table(length, -1.0)
    pixel_total = lax.psum(jnp.sum(foreground).astype(jnp.float32), ("img", "row"))
    inv_count = 1.0 / pixel_total
    middle_low = middle_weight.astype(jnp.bfloat16)
    conv_weights = [
        first_weight.astype(jnp.bfloat16),
        middle_low[0],
        middle_low[1],
        middle_low[2],
        last_weight.astype(jnp.bfloat16),
    ]
    penalty = jnp.exp(extra_params[2])
    offset = extra_params[:2]
    images_here = kspace.shape[1]
    pixels = images_here * kspace.shape[4] * length * lax.axis_size("img") * lax.axis_size("row")
    first_grad = jnp.zeros_like(first_weight)
    middle_grad = jnp.zeros_like(middle_weight)
    last_grad = jnp.zeros_like(last_weight)
    gains_grad = jnp.zeros_like(norm_gains)
    shifts_grad = jnp.zeros_like(norm_shifts)
    offset_grad = jnp.zeros((2,), jnp.float32)
    penalty_grad = jnp.float32(0.0)
    loss_part = jnp.float32(0.0)
    for microbatch in range(kspace.shape[0]):
        limit = jnp.where(anatomy[microbatch] == 0, BRAIN_COILS, COILS)
        coil_on = (jnp.arange(kspace.shape[2])[None, :] < limit[:, None]).astype(jnp.float32)
        maps = coil_maps[microbatch] * coil_on[:, :, None, None, None]
        mask_rows = row_mask[microbatch].astype(jnp.float32)[:, None, None, :, None]
        measured = to_columns(along_width(kspace[microbatch], inverse))
        normal, zero_filled = make_normal(maps, mask_rows, forward, inverse, measured)
        state = zero_filled
        unroll = 0
        denoised, cnn_kept = cnn_forward(
            state, conv_weights, norm_gains, norm_shifts, offset, pixels
        )
        rhs = zero_filled + penalty * denoised
        state, cg_kept = solve(rhs, penalty, normal)
        saved = [(cnn_kept, cg_kept, rhs, denoised)]
        fg_mask = foreground[microbatch].astype(jnp.float32)[:, None]
        difference = state - target[microbatch]
        loss_part = loss_part + jnp.sum(fg_mask * difference * difference)
        state_grad = inv_count * 2.0 * fg_mask * difference
        for unroll in reversed(range(UNROLLS)):
            cnn_kept, cg_kept, rhs, denoised = saved[unroll]
            denoised_grad, penalty_part = solve_backward(
                state_grad, cg_kept, rhs, denoised, penalty, normal
            )
            penalty_grad = penalty_grad + penalty_part
            state_grad, weight_grads, gain_part, shift_part, offset_part = cnn_backward(
                denoised_grad, cnn_kept, conv_weights, norm_gains, pixels, unroll > 0
            )
            first_grad = first_grad + weight_grads[0]
            middle_grad = middle_grad + jnp.stack(weight_grads[1:4])
            last_grad = last_grad + weight_grads[4]
            gains_grad = gains_grad + gain_part
            shifts_grad = shifts_grad + shift_part
            offset_grad = offset_grad + offset_part
    extra_grad = jnp.concatenate([offset_grad, (penalty * penalty_grad)[None]])
    totals = lax.psum(
        (first_grad, middle_grad, last_grad, gains_grad, shifts_grad, extra_grad, loss_part),
        ("img", "row"),
    )
    params = (first_weight, middle_weight, last_weight, norm_gains, norm_shifts, extra_params)
    moments = (
        (first_mean, first_square),
        (middle_mean, middle_square),
        (last_mean, last_square),
        (gains_mean, gains_square),
        (shifts_mean, shifts_square),
        (extra_mean, extra_square),
    )
    results = []
    for group in range(6):
        updated, first_new, second_new = adamw(
            params[group], totals[group], moments[group][0], moments[group][1], LEARN_RATES[group]
        )
        results.extend([updated, first_new, second_new])
        if group < 3:
            results.append(updated.astype(jnp.bfloat16))
    return tuple(results) + (totals[6], pixel_total.astype(jnp.int32))


def solution(mesh):
    in_specs = (
        P(None, "img", None, None, "row", None),
        P(None, "img", None, None, "row", None),
        P(None, "img", None, "row", None),
        P(None, "img", None),
        P(None, "img", "row", None),
        P(None, "img"),
        P(),
        P(),
        P(),
        P(),
        P(),
        P(),
        P(),
        P(),
        P(),
        P(),
        P(),
        P(),
        P(),
        P(),
        P(),
        P(),
        P(),
        P(),
    )
    out_specs = (
        P(),
        P(),
        P(),
        P(),
        P(),
        P(),
        P(),
        P(),
        P(),
        P(),
        P(),
        P(),
        P(),
        P(),
        P(),
        P(),
        P(),
        P(),
        P(),
        P(),
        P(),
        P(),
        P(),
    )
    return jax.shard_map(local, mesh=mesh, in_specs=in_specs, out_specs=out_specs, check_vma=False)
```

profile of v0, /device:TPU:0, one launch (start us, length us, event | category | flops | bytes accessed | tf_op | source)
XLA Modules:
  0.0 2391.4 jit_solution(6969696531948736520)
XLA Ops:
  16.5 6.0 fusion.557
  33.3 6.3 all-to-all-start
  39.6 8.9 fusion.591
  81.3 8.4 fusion.562
  121.5 8.4 fusion.596
  173.7 6.0 reshape.3447
  238.0 10.2 fusion.1414
  248.2 12.4 fusion.1415
  260.6 42.8 %all-reduce.30 = (f32[64]{0:T(128)S(1)}, f32[64]{0:T(128)S(1)}) all-reduce(f32[64]{0:T(128)S(1)} %get-tuple-element.329, f32[64]{0:T(128)S(1)} %get-tuple-element.331), channel_id=1, replica_groups=mesh['img'=4,'row'=8] {'img','row'}, use_global_device_ids=true, to_apply=%region_3.4 | all-reduce | flops 128 | bytes 1024 | tf_op jit(solution)/shard_map/psum | solution.py:218
  307.4 40.0 %all-reduce.29 = (f32[64]{0:T(128)S(1)}, f32[64]{0:T(128)S(1)}) all-reduce(f32[64]{0:T(128)S(1)} %multiply_reduce_fusion.7, f32[64]{0:T(128)S(1)} %multiply_reduce_fusion.3), channel_id=1, replica_groups=mesh['img'=4,'row'=8] {'img','row'}, use_global_device_ids=true, to_apply=%region_5.6 | all-reduce | flops 128 | bytes 1024 | tf_op jit(solution)/shard_map/psum | solution.py:218
  400.4 11.5 fusion.1417
  412.0 12.3 fusion.1416
  424.3 43.5 %all-reduce.28 = (f32[64]{0:T(128)S(1)}, f32[64]{0:T(128)S(1)}) all-reduce(f32[64]{0:T(128)S(1)} %get-tuple-element.333, f32[64]{0:T(128)S(1)} %get-tuple-element.335), channel_id=1, replica_groups=mesh['img'=4,'row'=8] {'img','row'}, use_global_device_ids=true, to_apply=%region_7.8 | all-reduce | flops 128 | bytes 1024 | tf_op jit(solution)/shard_map/psum | solution.py:218
  471.8 40.0 %all-reduce.27 = (f32[64]{0:T(128)S(1)}, f32[64]{0:T(128)S(1)}) all-reduce(f32[64]{0:T(128)S(1)} %multiply_reduce_fusion.6, f32[64]{0:T(128)S(1)} %multiply_reduce_fusion.2), channel_id=1, replica_groups=mesh['img'=4,'row'=8] {'img','row'}, use_global_device_ids=true, to_apply=%region_9.10 | all-reduce | flops 128 | bytes 1024 | tf_op jit(solution)/shard_map/psum | solution.py:218
  565.1 11.4 fusion.1419
  576.5 12.3 fusion.1418
  588.8 43.4 %all-reduce.26 = (f32[64]{0:T(128)S(1)}, f32[64]{0:T(128)S(1)}) all-reduce(f32[64]{0:T(128)S(1)} %get-tuple-element.337, f32[64]{0:T(128)S(1)} %get-tuple-element.339), channel_id=1, replica_groups=mesh['img'=4,'row'=8] {'img','row'}, use_global_device_ids=true, to_apply=%region_11.12 | all-reduce | flops 128 | bytes 1024 | tf_op jit(solution)/shard_map/psum | solution.py:218
  636.2 40.1 %all-reduce.25 = (f32[64]{0:T(128)S(1)}, f32[64]{0:T(128)S(1)}) all-reduce(f32[64]{0:T(128)S(1)} %multiply_reduce_fusion.5, f32[64]{0:T(128)S(1)} %multiply_reduce_fusion.1), channel_id=1, replica_groups=mesh['img'=4,'row'=8] {'img','row'}, use_global_device_ids=true, to_apply=%region_13.14 | all-reduce | flops 128 | bytes 1024 | tf_op jit(solution)/shard_map/psum | solution.py:218
  729.4 11.7 fusion.1421
  741.1 12.3 fusion.1420
  753.5 43.3 %all-reduce.24 = (f32[64]{0:T(128)S(1)}, f32[64]{0:T(128)S(1)}) all-reduce(f32[64]{0:T(128)S(1)} %get-tuple-element.341, f32[64]{0:T(128)S(1)} %get-tuple-element.343), channel_id=1, replica_groups=mesh['img'=4,'row'=8] {'img','row'}, use_global_device_ids=true, to_apply=%region_15.16 | all-reduce | flops 128 | bytes 1024 | tf_op jit(solution)/shard_map/psum | solution.py:218
  800.8 40.2 %all-reduce.23 = (f32[64]{0:T(128)S(1)}, f32[]{:T(128)}, f32[64]{0:T(128)S(1)}) all-reduce(f32[64]{0:T(128)S(1)} %multiply_reduce_fusion.4, f32[]{:T(128)S(6)} %convert_element_type.527, f32[64]{0:T(128)S(1)} %multiply_reduce_fusion), channel_id=1, replica_groups=mesh['img'=4,'row'=8] {'img','row'}, use_global_device_ids=true, to_apply=%region_17.18 | all-reduce | flops 129 | bytes 1032 | tf_op jit(solution)/shard_map/psum | solution.py:218
  885.2 6.9 all-to-all-start.12
  900.2 6.1 fusion.567
  963.7 6.0 reshape.3429
  984.0 6.1 fusion.568
  1028.7 6.0 reshape.3431
  1051.0 15.2 all-reduce.35
  1070.6 14.3 all-reduce.34
  1111.7 6.1 fusion.573
  1175.1 6.0 reshape.3433
  1195.3 6.1 fusion.574
  1242.4 6.0 reshape.3435
  1265.4 17.8 all-reduce.33
  1291.2 14.9 all-reduce.32
  1312.7 6.1 fusion.613
  1343.5 6.1 fusion.579
  1385.7 6.1 fusion.614
  1409.0 6.0 reshape.3437
  1429.2 6.1 fusion.580
  1479.9 6.0 reshape.3439
  1504.3 17.9 all-reduce.31
  1529.2 6.1 fusion.585
  1563.5 6.1 fusion.619
  1607.6 6.1 fusion.586
  1662.8 6.1 fusion.620
  1710.1 6.0 reshape.3463
  1800.2 13.2 fusion.1370
  1813.5 13.0 fusion.1366
  1826.6 41.7 %all-reduce.22 = (f32[64]{0:T(128)S(1)}, f32[64]{0:T(128)S(1)}, f32[64]{0:T(128)S(1)}, f32[64]{0:T(128)S(1)}) all-reduce(f32[64]{0:T(128)S(1)} %get-tuple-element.48, f32[64]{0:T(128)S(1)} %get-tuple-element.47, f32[64]{0:T(128)S(1)} %get-tuple-element.30, f32[64]{0:T(128)S(1)} %get-tuple-element.29), channel_id=1, replica_groups=mesh['img'=4,'row'=8] {'img','row'}, use_global_device_ids=true, to_apply=%region_57.58 | all-reduce | flops 256 | bytes 2048 | tf_op jit(solution)/shard_map/psum | solution.py:257
  1868.3 6.8 fusion.13
  1947.5 14.6 fusion.1369
  1962.2 14.2 fusion.1365
  1976.4 41.2 %all-reduce.21 = (f32[64]{0:T(128)S(1)}, f32[64]{0:T(128)S(1)}, f32[64]{0:T(128)S(1)}, f32[64]{0:T(128)S(1)}) all-reduce(f32[64]{0:T(128)S(1)} %get-tuple-element.46, f32[64]{0:T(128)S(1)} %get-tuple-element.45, f32[64]{0:T(128)S(1)} %get-tuple-element.28, f32[64]{0:T(128)S(1)} %get-tuple-element.27), channel_id=1, replica_groups=mesh['img'=4,'row'=8] {'img','row'}, use_global_device_ids=true, to_apply=%region_61.62 | all-reduce | flops 256 | bytes 2048 | tf_op jit(solution)/shard_map/psum | solution.py:257
  2017.6 6.8 fusion.18
  2096.1 14.4 fusion.1368
  2110.5 14.2 fusion.1364
  2124.8 40.9 %all-reduce.20 = (f32[64]{0:T(128)S(1)}, f32[64]{0:T(128)S(1)}, f32[64]{0:T(128)S(1)}, f32[64]{0:T(128)S(1)}) all-reduce(f32[64]{0:T(128)S(1)} %get-tuple-element.44, f32[64]{0:T(128)S(1)} %get-tuple-element.43, f32[64]{0:T(128)S(1)} %get-tuple-element.26, f32[64]{0:T(128)S(1)} %get-tuple-element.25), channel_id=1, replica_groups=mesh['img'=4,'row'=8] {'img','row'}, use_global_device_ids=true, to_apply=%region_65.66 | all-reduce | flops 256 | bytes 2048 | tf_op jit(solution)/shard_map/psum | solution.py:257
  2165.7 7.3 fusion.23
  2247.0 14.2 fusion.1367
  2261.3 15.4 fusion.1363
  2276.7 40.9 %all-reduce.19 = (f32[64]{0:T(128)S(1)}, f32[64]{0:T(128)S(1)}, f32[64]{0:T(128)S(1)}, f32[64]{0:T(128)S(1)}) all-reduce(f32[64]{0:T(128)S(1)} %get-tuple-element.42, f32[64]{0:T(128)S(1)} %get-tuple-element.41, f32[64]{0:T(128)S(1)} %get-tuple-element.24, f32[64]{0:T(128)S(1)} %get-tuple-element.23), channel_id=1, replica_groups=mesh['img'=4,'row'=8] {'img','row'}, use_global_device_ids=true, to_apply=%region_69.70 | all-reduce | flops 256 | bytes 2048 | tf_op jit(solution)/shard_map/psum | solution.py:257
  2317.6 6.8 fusion.88
  2336.9 39.8 %all-reduce.18 = (f32[9,64,2]{1,2,0:T(2,128)S(1)}, f32[9,2,64]{2,1,0:T(2,128)S(1)}, f32[4,64]{1,0:T(4,128)S(1)}, f32[4,64]{1,0:T(4,128)S(1)}, f32[3]{0:T(128)S(1)}, /*index=5*/f32[]{:T(128)}) all-reduce(f32[9,64,2]{1,2,0:T(2,128)S(1)} %add.1731, f32[9,2,64]{2,1,0:T(2,128)S(1)} %copy-done.207, ...), channel_id=1, replica_groups=mesh['img'=4,'row'=8] {'img','row'}, use_global_device_ids=true, to_apply=%region_138.139 | all-reduce | flops 2820 | bytes 22560 | tf_op jit(solution)/shard_map/psum | solution.py:371
  (1283 shorter events, 1298.5 us)
Async XLA Ops:
  33.3 28.0 %all-to-all-start = ((bf16[8,2,25600]{2,1,0:T(2,128)(2,1)}), bf16[8,2,25600]{2,1,0:T(2,128)(2,1)S(1)}, u32[]{:S(2)}, u32[]{:S(2)}) async-start(bf16[8,2,25600]{2,1,0:T(2,128)(2,1)} %reshape.3424), calls=%async_computation | async-start | bytes 1638400 | tf_op jit(solution)/shard_map/all_to_all | solution.py:77
  62.2 38.0 %all-to-all-start.10 = ((bf16[8,2,25600]{2,1,0:T(2,128)(2,1)}), bf16[8,2,25600]{2,1,0:T(2,128)(2,1)S(1)}, u32[]{:S(2)}, u32[]{:S(2)}) async-start(bf16[8,2,25600]{2,1,0:T(2,128)(2,1)} %reshape.3444), calls=%async_computation.10 | async-start | bytes 1638400 | tf_op jit(solution)/shard_map/all_to_all | solution.py:77
  101.1 39.3 %all-to-all-start.1 = ((bf16[8,2,25600]{2,1,0:T(2,128)(2,1)}), bf16[8,2,25600]{2,1,0:T(2,128)(2,1)S(1)}, u32[]{:S(2)}, u32[]{:S(2)}) async-start(bf16[8,2,25600]{2,1,0:T(2,128)(2,1)} %reshape.3426), calls=%async_computation.1 | async-start | bytes 1638400 | tf_op jit(solution)/shard_map/all_to_all | solution.py:83
  140.5 33.2 %all-to-all-start.11 = ((bf16[8,2,25600]{2,1,0:T(2,128)(2,1)}), bf16[8,2,25600]{2,1,0:T(2,128)(2,1)}, u32[]{:S(2)}, u32[]{:S(2)}) async-start(bf16[8,2,25600]{2,1,0:T(2,128)(2,1)} %reshape.3446), calls=%async_computation.11 | async-start | bytes 1638400 | tf_op jit(solution)/shard_map/all_to_all | solution.py:83
  148.0 593.1 %copy-start.51 = (bf16[3,9,64,64]{3,2,1,0:T(8,128)(2,1)}, bf16[3,9,64,64]{3,2,1,0:T(8,128)(2,1)S(1)}, u32[]{:S(2)}) copy-start(bf16[3,9,64,64]{3,2,1,0:T(8,128)(2,1)S(1)} %convert_element_type.510) | copy-start | bytes 663556
  151.8 195.7 %copy-start.219 = (f32[64]{0:T(128)}, f32[64]{0:T(128)S(1)}, u32[]{:S(2)}) copy-start(f32[64]{0:T(128)S(1)} %get-tuple-element.363) | copy-start | bytes 772
  151.8 195.7 %copy-start.263 = (f32[64]{0:T(128)}, f32[64]{0:T(128)S(1)}, u32[]{:S(2)}) copy-start(f32[64]{0:T(128)S(1)} %get-tuple-element.310) | copy-start | bytes 772
  151.8 360.1 %copy-start.221 = (f32[64]{0:T(128)}, f32[64]{0:T(128)S(1)}, u32[]{:S(2)}) copy-start(f32[64]{0:T(128)S(1)} %get-tuple-element.364) | copy-start | bytes 772
  151.8 360.1 %copy-start.265 = (f32[64]{0:T(128)}, f32[64]{0:T(128)S(1)}, u32[]{:S(2)}) copy-start(f32[64]{0:T(128)S(1)} %get-tuple-element.309) | copy-start | bytes 772
  192.5 11.5 collective-permute-start
  194.9 9.1 collective-permute-start.1
  196.4 19.9 collective-permute-start.18
  200.6 15.7 collective-permute-start.19
  352.5 9.3 collective-permute-start.20
  353.8 8.0 collective-permute-start.21
  356.4 21.4 collective-permute-start.2
  360.3 17.6 collective-permute-start.3
  517.5 8.9 collective-permute-start.22
  518.8 7.6 collective-permute-start.23
  520.8 21.6 collective-permute-start.4
  524.7 17.7 collective-permute-start.5
  681.3 59.8 %copy-start.40 = (bf16[1,64,40,320]{3,1,2,0:T(8,128)(2,1)}, bf16[1,64,40,320]{3,1,2,0:T(8,128)(2,1)S(1)}, u32[]{:S(2)}) copy-start(bf16[1,64,40,320]{3,1,2,0:T(8,128)(2,1)S(1)} %get-tuple-element.314) | copy-start | bytes 4915204
  682.0 8.7 collective-permute-start.24
  683.3 7.4 collective-permute-start.25
  685.3 21.5 collective-permute-start.6
  689.2 17.6 collective-permute-start.7
  846.1 8.8 collective-permute-start.26
  847.4 7.5 collective-permute-start.27
  849.4 9.2 collective-permute-start.8
  853.3 5.3 collective-permute-start.9
  885.2 32.7 %all-to-all-start.12 = ((bf16[8,2,25600]{2,1,0:T(2,128)(2,1)}), bf16[8,2,25600]{2,1,0:T(2,128)(2,1)S(1)}, u32[]{:S(2)}, u32[]{:S(2)}) async-start(bf16[8,2,25600]{2,1,0:T(2,128)(2,1)} %reshape.3448), calls=%async_computation.12 | async-start | bytes 1638400 | tf_op jit(solution)/shard_map/all_to_all | solution.py:77
  918.0 40.2 %all-to-all-start.2 = ((bf16[8,2,25600]{2,1,0:T(2,128)(2,1)}), bf16[8,2,25600]{2,1,0:T(2,128)(2,1)}, u32[]{:S(2)}, u32[]{:S(2)}) async-start(bf16[8,2,25600]{2,1,0:T(2,128)(2,1)} %reshape.3428), calls=%async_computation.2 | async-start | bytes 1638400 | tf_op jit(solution)/shard_map/all_to_all | solution.py:77
  958.2 43.6 %all-to-all-start.13 = ((bf16[8,2,25600]{2,1,0:T(2,128)(2,1)}), bf16[8,2,25600]{2,1,0:T(2,128)(2,1)S(1)}, u32[]{:S(2)}, u32[]{:S(2)}) async-start(bf16[8,2,25600]{2,1,0:T(2,128)(2,1)} %reshape.3450), calls=%async_computation.13 | async-start | bytes 1638400 | tf_op jit(solution)/shard_map/all_to_all | solution.py:83
  1001.8 26.9 %all-to-all-start.3 = ((bf16[8,2,25600]{2,1,0:T(2,128)(2,1)}), bf16[8,2,25600]{2,1,0:T(2,128)(2,1)}, u32[]{:S(2)}, u32[]{:S(2)}) async-start(bf16[8,2,25600]{2,1,0:T(2,128)(2,1)} %reshape.3430), calls=%async_computation.3 | async-start | bytes 1638400 | tf_op jit(solution)/shard_map/all_to_all | solution.py:83
  1103.9 25.6 %all-to-all-start.14 = ((bf16[8,2,25600]{2,1,0:T(2,128)(2,1)}), bf16[8,2,25600]{2,1,0:T(2,128)(2,1)S(1)}, u32[]{:S(2)}, u32[]{:S(2)}) async-start(bf16[8,2,25600]{2,1,0:T(2,128)(2,1)} %reshape.3452), calls=%async_computation.14 | async-start | bytes 1638400 | tf_op jit(solution)/shard_map/all_to_all | solution.py:77
  1129.5 40.1 %all-to-all-start.4 = ((bf16[8,2,25600]{2,1,0:T(2,128)(2,1)}), bf16[8,2,25600]{2,1,0:T(2,128)(2,1)}, u32[]{:S(2)}, u32[]{:S(2)}) async-start(bf16[8,2,25600]{2,1,0:T(2,128)(2,1)} %reshape.3432), calls=%async_computation.4 | async-start | bytes 1638400 | tf_op jit(solution)/shard_map/all_to_all | solution.py:77
  1169.6 43.6 %all-to-all-start.15 = ((bf16[8,2,25600]{2,1,0:T(2,128)(2,1)}), bf16[8,2,25600]{2,1,0:T(2,128)(2,1)S(1)}, u32[]{:S(2)}, u32[]{:S(2)}) async-start(bf16[8,2,25600]{2,1,0:T(2,128)(2,1)} %reshape.3454), calls=%async_computation.15 | async-start | bytes 1638400 | tf_op jit(solution)/shard_map/all_to_all | solution.py:83
  1213.2 29.2 %all-to-all-start.5 = ((bf16[8,2,25600]{2,1,0:T(2,128)(2,1)}), bf16[8,2,25600]{2,1,0:T(2,128)(2,1)}, u32[]{:S(2)}, u32[]{:S(2)}) async-start(bf16[8,2,25600]{2,1,0:T(2,128)(2,1)} %reshape.3434), calls=%async_computation.5 | async-start | bytes 1638400 | tf_op jit(solution)/shard_map/all_to_all | solution.py:83
  1222.0 65.1 %copy-start.135 = (f32[40,320]{1,0:T(8,128)}, f32[40,320]{1,0:T(8,128)S(1)}, u32[]{:S(2)}) copy-start(f32[40,320]{1,0:T(8,128)S(1)} %get-tuple-element.264) | copy-start | bytes 153604
  1330.5 30.8 %all-to-all-start.16 = ((bf16[8,2,25600]{2,1,0:T(2,128)(2,1)}), bf16[8,2,25600]{2,1,0:T(2,128)(2,1)S(1)}, u32[]{:S(2)}, u32[]{:S(2)}) async-start(bf16[8,2,25600]{2,1,0:T(2,128)(2,1)} %reshape.3456), calls=%async_computation.16 | async-start | bytes 1638400 | tf_op jit(solution)/shard_map/all_to_all | solution.py:77
  1361.3 42.2 %all-to-all-start.6 = ((bf16[8,2,25600]{2,1,0:T(2,128)(2,1)}), bf16[8,2,25600]{2,1,0:T(2,128)(2,1)}, u32[]{:S(2)}, u32[]{:S(2)}) async-start(bf16[8,2,25600]{2,1,0:T(2,128)(2,1)} %reshape.3436), calls=%async_computation.6 | async-start | bytes 1638400 | tf_op jit(solution)/shard_map/all_to_all | solution.py:77
  1403.4 43.6 %all-to-all-start.17 = ((bf16[8,2,25600]{2,1,0:T(2,128)(2,1)}), bf16[8,2,25600]{2,1,0:T(2,128)(2,1)S(1)}, u32[]{:S(2)}, u32[]{:S(2)}) async-start(bf16[8,2,25600]{2,1,0:T(2,128)(2,1)} %reshape.3458), calls=%async_computation.17 | async-start | bytes 1638400 | tf_op jit(solution)/shard_map/all_to_all | solution.py:83
  1447.0 32.9 %all-to-all-start.7 = ((bf16[8,2,25600]{2,1,0:T(2,128)(2,1)}), bf16[8,2,25600]{2,1,0:T(2,128)(2,1)}, u32[]{:S(2)}, u32[]{:S(2)}) async-start(bf16[8,2,25600]{2,1,0:T(2,128)(2,1)} %reshape.3438), calls=%async_computation.7 | async-start | bytes 1638400 | tf_op jit(solution)/shard_map/all_to_all | solution.py:83
  1547.0 34.2 %all-to-all-start.8 = ((bf16[8,2,25600]{2,1,0:T(2,128)(2,1)}), bf16[8,2,25600]{2,1,0:T(2,128)(2,1)S(1)}, u32[]{:S(2)}, u32[]{:S(2)}) async-start(bf16[8,2,25600]{2,1,0:T(2,128)(2,1)} %reshape.3440), calls=%async_computation.8 | async-start | bytes 1638400 | tf_op jit(solution)/shard_map/all_to_all | solution.py:77
  1582.1 43.2 %all-to-all-start.18 = ((bf16[8,2,25600]{2,1,0:T(2,128)(2,1)}), bf16[8,2,25600]{2,1,0:T(2,128)(2,1)S(1)}, u32[]{:S(2)}, u32[]{:S(2)}) async-start(bf16[8,2,25600]{2,1,0:T(2,128)(2,1)} %reshape.3460), calls=%async_computation.18 | async-start | bytes 1638400 | tf_op jit(solution)/shard_map/all_to_all | solution.py:77
  1626.2 54.4 %all-to-all-start.9 = ((bf16[8,2,25600]{2,1,0:T(2,128)(2,1)}), bf16[8,2,25600]{2,1,0:T(2,128)(2,1)S(1)}, u32[]{:S(2)}, u32[]{:S(2)}) async-start(bf16[8,2,25600]{2,1,0:T(2,128)(2,1)} %reshape.3442), calls=%async_computation.9 | async-start | bytes 1638400 | tf_op jit(solution)/shard_map/all_to_all | solution.py:83
  1680.6 29.4 %all-to-all-start.19 = ((bf16[8,2,25600]{2,1,0:T(2,128)(2,1)}), bf16[8,2,25600]{2,1,0:T(2,128)(2,1)}, u32[]{:S(2)}, u32[]{:S(2)}) async-start(bf16[8,2,25600]{2,1,0:T(2,128)(2,1)} %reshape.3462), calls=%async_computation.19 | async-start | bytes 1638400 | tf_op jit(solution)/shard_map/all_to_all | solution.py:83
  1685.7 694.0 %all-reduce.38.cloned.1.call-start = ((), (), s32[]{:S(2)}) async-start(), calls=%async_computation.20 | async-start | bytes 1769472 | tf_op jit(solution)/shard_map/psum | solution.py:371
  1736.9 25.3 %collective-permute-start.11 = (bf16[1,2,1,320]{3,1,2,0:T(2,128)(2,1)S(1)}, bf16[1,2,1,320]{3,1,2,0:T(2,128)(2,1)S(1)}, u32[]{:S(2)}, u32[]{:S(2)}) collective-permute-start(bf16[1,2,1,320]{3,1,2,0:T(2,128)(2,1)S(1)} %get-tuple-element.282), channel_id=1, source_target_pairs={{1,0},{2,1},{3,2},{4,3},{5,4},{6,5},{7,6},{9,8},{10,9},{11,10},{12... | collective-permute-start | bytes 3848 | tf_op jit(solution)/shard_map/ppermute | solution.py:32
  1738.2 24.0 %collective-permute-start.10 = (bf16[1,2,1,320]{3,1,2,0:T(2,128)(2,1)S(1)}, bf16[1,2,1,320]{3,1,2,0:T(2,128)(2,1)S(1)}, u32[]{:S(2)}, u32[]{:S(2)}) collective-permute-start(bf16[1,2,1,320]{3,1,2,0:T(2,128)(2,1)S(1)} %get-tuple-element.281), channel_id=1, source_target_pairs={{0,1},{1,2},{2,3},{3,4},{4,5},{5,6},{6,7},{8,9},{9,10},{10,11},{11... | collective-permute-start | bytes 3848 | tf_op jit(solution)/shard_map/ppermute | solution.py:30
  1741.2 36.9 %collective-permute-start.29 = (bf16[1,2,1,320]{3,1,2,0:T(2,128)(2,1)S(1)}, bf16[1,2,1,320]{3,1,2,0:T(2,128)(2,1)S(1)}, u32[]{:S(2)}, u32[]{:S(2)}) collective-permute-start(bf16[1,2,1,320]{3,1,2,0:T(2,128)(2,1)S(1)} %get-tuple-element.280), channel_id=1, source_target_pairs={{1,0},{2,1},{3,2},{4,3},{5,4},{6,5},{7,6},{9,8},{10,9},{11,10},{12... | collective-permute-start | bytes 3848 | tf_op jit(solution)/shard_map/ppermute | solution.py:32
  1742.5 35.6 %collective-permute-start.28 = (bf16[1,2,1,320]{3,1,2,0:T(2,128)(2,1)S(1)}, bf16[1,2,1,320]{3,1,2,0:T(2,128)(2,1)S(1)}, u32[]{:S(2)}, u32[]{:S(2)}) collective-permute-start(bf16[1,2,1,320]{3,1,2,0:T(2,128)(2,1)S(1)} %get-tuple-element.279), channel_id=1, source_target_pairs={{0,1},{1,2},{2,3},{3,4},{4,5},{5,6},{6,7},{8,9},{9,10},{10,11},{11... | collective-permute-start | bytes 3848 | tf_op jit(solution)/shard_map/ppermute | solution.py:30
  1882.8 23.0 collective-permute-start.13
  1884.1 21.7 collective-permute-start.12
  1887.2 36.7 %collective-permute-start.31 = (bf16[1,64,1,320]{3,1,2,0:T(8,128)(2,1)S(1)}, bf16[1,64,1,320]{3,1,2,0:T(8,128)(2,1)S(1)}, u32[]{:S(2)}, u32[]{:S(2)}) collective-permute-start(bf16[1,64,1,320]{3,1,2,0:T(8,128)(2,1)S(1)} %get-tuple-element.224), channel_id=1, source_target_pairs={{1,0},{2,1},{3,2},{4,3},{5,4},{6,5},{7,6},{9,8},{10,9},{11,10},{12... | collective-permute-start | bytes 122888 | tf_op jit(solution)/shard_map/ppermute | solution.py:32
  1888.5 35.4 %collective-permute-start.30 = (bf16[1,64,1,320]{3,1,2,0:T(8,128)(2,1)S(1)}, bf16[1,64,1,320]{3,1,2,0:T(8,128)(2,1)S(1)}, u32[]{:S(2)}, u32[]{:S(2)}) collective-permute-start(bf16[1,64,1,320]{3,1,2,0:T(8,128)(2,1)S(1)} %get-tuple-element.223), channel_id=1, source_target_pairs={{0,1},{1,2},{2,3},{3,4},{4,5},{5,6},{6,7},{8,9},{9,10},{10,11},{11... | collective-permute-start | bytes 122888 | tf_op jit(solution)/shard_map/ppermute | solution.py:30
  2032.0 22.6 collective-permute-start.15
  2033.3 21.3 collective-permute-start.14
  2036.4 36.1 %collective-permute-start.33 = (bf16[1,64,1,320]{3,1,2,0:T(8,128)(2,1)S(1)}, bf16[1,64,1,320]{3,1,2,0:T(8,128)(2,1)S(1)}, u32[]{:S(2)}, u32[]{:S(2)}) collective-permute-start(bf16[1,64,1,320]{3,1,2,0:T(8,128)(2,1)S(1)} %get-tuple-element.220), channel_id=1, source_target_pairs={{1,0},{2,1},{3,2},{4,3},{5,4},{6,5},{7,6},{9,8},{10,9},{11,10},{12... | collective-permute-start | bytes 122888 | tf_op jit(solution)/shard_map/ppermute | solution.py:32
  2037.7 34.8 %collective-permute-start.32 = (bf16[1,64,1,320]{3,1,2,0:T(8,128)(2,1)S(1)}, bf16[1,64,1,320]{3,1,2,0:T(8,128)(2,1)S(1)}, u32[]{:S(2)}, u32[]{:S(2)}) collective-permute-start(bf16[1,64,1,320]{3,1,2,0:T(8,128)(2,1)S(1)} %get-tuple-element.219), channel_id=1, source_target_pairs={{0,1},{1,2},{2,3},{3,4},{4,5},{5,6},{6,7},{8,9},{9,10},{10,11},{11... | collective-permute-start | bytes 122888 | tf_op jit(solution)/shard_map/ppermute | solution.py:30
  2194.1 9.8 collective-permute-start.17
  2195.4 8.5 collective-permute-start.16
  2199.5 23.6 collective-permute-start.35
  2200.8 22.3 collective-permute-start.34
  (309 other events, 3916.2 us)
Sparse Core Ops, SparseCore 0:
  2199.6 128.9 all-reduce.37
where the time goes:
time: 2410 us; the launch traced here: 2390 us
  matrix products  803 us (33%)
  blocking collectives  618 us (26%)
  local copies, waits for them, and re-layouts  566 us (23%)
  starting transfers between devices  182 us (8%)
  other arithmetic  142 us (6%)
  between operations  74.1 us (3%)
    psum x8, blocking collectives, norm_sums(): return lax.psum(values, ('img', 'row'))  333 us
    dot_general x72, matrix products, conv_backward(): jnp.einsum('oi,borw->birw', weight[tap_index], window, preferred_element_...  286 us
    unnamed x688, local copies, waits for them, and re-layouts  254 us
    dot_general x90, matrix products, conv_forward(): jnp.einsum('oi,birw->borw', weight[tap_index], window, preferred_element_...  253 us
    psum x4, blocking collectives, cnn_backward(): lax.psum((shift_local, gain_local), ('img', 'row'))  165 us
    dot_general x18, matrix products, along_height(): return jnp.einsum('bcprw,prqk->bcqkw', field, table, precision=PRECISE)  101 us
    dot_general x18, matrix products, along_width(): return jnp.einsum('bcprw,pwqk->bcqrk', field, table, precision=PRECISE)  98.1 us
    another operation x16, local copies, waits for them, and re-layouts  73.3 us
  transfers between devices with their start and end apart: 57, of which 3 were waited for; matrix products, arithmetic and copies ran while one was open for 35% of the time, Pallas kernels for 0%

commit v1 on v0

--- a/solution.py
+++ b/solution.py
@@ -1,6 +1,11 @@
+import functools
+
 import jax
 import jax.numpy as jnp
+import numpy as np
 from jax import lax
+from jax.experimental import pallas as pl
+from jax.experimental.pallas import tpu as pltpu
 from jax.sharding import PartitionSpec as P
 
 COILS = 16
@@ -282,32 +287,10 @@
     return (updated, first_new, second_new)
 
 
-def local(
-    kspace,
-    coil_maps,
-    target,
-    row_mask,
-    foreground,
-    anatomy,
-    first_weight,
-    middle_weight,
-    last_weight,
-    norm_gains,
-    norm_shifts,
-    extra_params,
-    first_mean,
-    first_square,
-    middle_mean,
-    middle_square,
-    last_mean,
-    last_square,
-    gains_mean,
-    gains_square,
-    shifts_mean,
-    shifts_square,
-    extra_mean,
-    extra_square,
-):
+def general_local(arrays):
+    (
+        kspace, coil_maps, target, row_mask, foreground, anatomy, first_weight, middle_weight, last_weight, norm_gains, norm_shifts, extra_params,
+    ) = arrays
     length = kspace.shape[-1]
     forward = dft_table(length, 1.0)
     inverse = dft_table(length, -1.0)
@@ -372,6 +355,1175 @@
         (first_grad, middle_grad, last_grad, gains_grad, shifts_grad, extra_grad, loss_part),
         ("img", "row"),
     )
+    return totals, pixel_total
+
+
+BF16 = jnp.bfloat16
+F32 = jnp.float32
+MESH = pl.DeviceIdType.MESH
+TILE = 128
+BLOCK = 8
+VMEM_BYTES = 58 * 1024 * 1024
+
+
+def padded(length):
+    return -(-length // TILE) * TILE
+
+
+def fits(kspace, first_weight, mesh_rows):
+    micro, images, coils, _, rows, length = kspace.shape
+    channels = first_weight.shape[1]
+    return (
+        images == 1
+        and micro * channels == TILE
+        and channels % 16 == 0
+        and rows * mesh_rows == length
+        and rows % BLOCK == 0
+        and (2 * rows) % 16 == 0
+        and (coils * rows) % TILE == 0
+        and padded(length) > length
+    )
+
+
+def phases(length):
+    index = np.arange(length)
+    angle = 2.0 * np.pi * (np.outer(index, index) % length) / length
+    return np.cos(angle) / np.sqrt(length), np.sin(angle) / np.sqrt(length)
+
+
+def high_low(table):
+    high = table.astype(BF16)
+    low = (table - high.astype(F32)).astype(BF16)
+    return high, low
+
+
+def np_high_low(table):
+    table = np.asarray(table, np.float32)
+    high = table.astype(BF16)
+    low = (table - high.astype(np.float32)).astype(BF16)
+    return jnp.asarray(high), jnp.asarray(low)
+
+
+def dot(left, right):
+    return jnp.dot(left, right, preferred_element_type=F32)
+
+
+def dot_nt(left, right):
+    return lax.dot_general(left, right, (((1,), (1,)), ((), ())), preferred_element_type=F32)
+
+
+def greet(peers):
+    barrier = pltpu.get_barrier_semaphore()
+    for peer in peers:
+        pl.semaphore_signal(barrier, inc=1, device_id=peer, device_id_type=MESH)
+    pl.semaphore_wait(barrier, len(peers))
+
+
+def row_peers(rows):
+    image, row = lax.axis_index("img"), lax.axis_index("row")
+    return [(image, lax.rem(row + step, rows)) for step in range(1, rows)]
+
+
+def image_peers(images):
+    image, row = lax.axis_index("img"), lax.axis_index("row")
+    return [(lax.rem(image + step, images), row) for step in range(1, images)]
+
+
+def remote(source, target, send, receive, peer):
+    copy = pltpu.make_async_remote_copy(
+        src_ref=source,
+        dst_ref=target,
+        send_sem=send,
+        recv_sem=receive,
+        device_id=peer,
+        device_id_type=MESH,
+    )
+    copy.start()
+    return copy
+
+
+def params(vmem=VMEM_BYTES, **kwargs):
+    return pltpu.CompilerParams(vmem_limit_bytes=vmem, **kwargs)
+
+
+def in_vmem():
+    return pl.BlockSpec(memory_space=pltpu.VMEM)
+
+
+def anywhere():
+    return pl.BlockSpec(memory_space=pl.ANY)
+
+
+def exchange_kernel(
+    sizes, kspace, maps, turn_high, turn_low, pick, mask, cosine, sine, spread, normal_high, normal_low, staged, send, receive, own
+):
+    micro, coils, rows, length, parts = sizes
+    wide = padded(length)
+    image, me = lax.axis_index("img"), lax.axis_index("row")
+    peers = row_peers(parts)
+    greet(peers)
+    copies = []
+    slabs = 2 * rows
+    for batch in range(micro):
+        for kind in range(2):
+            total = None
+            for part in range(2):
+                source = (kspace, maps)[kind]
+                field = source[batch, :, part].reshape(coils * rows, length)
+                if kind == 0:
+                    high, low = high_low(field)
+                    term = (
+                        dot_nt(turn_high[part], high)
+                        + dot_nt(turn_low[part], high)
+                        + dot_nt(turn_high[part], low)
+                    )
+                else:
+                    term = dot_nt(pick[part], field.astype(BF16))
+                total = term if total is None else total + term
+            slot = 2 * batch + kind
+            staged[slot] = total.astype(BF16).reshape(parts, slabs, coils * rows)
+            local = pltpu.make_async_copy(staged.at[slot, me], spread.at[slot, me], own.at[slot])
+            local.start()
+            copies.append(local)
+            order = sorted(range(1, parts), key=lambda step: -min(step, parts - step))
+            for step in order:
+                peer = peers[step - 1]
+                copies.append(
+                    remote(
+                        staged.at[slot, peer[1]],
+                        spread.at[slot, me],
+                        send.at[slot, step - 1],
+                        receive.at[slot, step - 1],
+                        peer,
+                    )
+                )
+    for batch in range(micro):
+        chosen = mask[batch]
+        cos_on, sin_on = cosine[...] * chosen, sine[...] * chosen
+
+        def product(left, right):
+            return jnp.dot(left, right, precision=PRECISE, preferred_element_type=F32)
+
+        real = product(cos_on, cosine[...]) + product(sin_on, sine[...])
+        imag = product(sin_on, cosine[...]) - product(cos_on, sine[...])
+        for block, value in (((0, 0), real), ((0, 1), -imag), ((1, 0), imag), ((1, 1), real)):
+            high, low = high_low(value)
+            at = (batch, pl.ds(block[0] * wide, wide), pl.ds(block[1] * wide, wide))
+            normal_high[at] = high
+            normal_low[at] = low
+    for copy in copies:
+        copy.wait()
+
+
+def exchange(kspace, maps, mask, parts):
+    micro, coils, _, rows, length = kspace.shape
+    wide = padded(length)
+    cosine, sine = phases(length)
+    inverse = np.stack([np.stack([cosine, sine], 0), np.stack([-sine, cosine], 0)], 0)
+    turn = inverse.reshape(2, 2, length, parts, rows).transpose(0, 3, 1, 4, 2).reshape(2, 2 * length, length)
+    pick = np.zeros((2, parts, 2, rows, length), np.float32)
+    for part in range(2):
+        for block in range(parts):
+            pick[part, block, part, :, block * rows : (block + 1) * rows] = np.eye(rows)
+    pick = jnp.asarray(pick.reshape(2, 2 * length, length).astype(BF16))
+    turn_high, turn_low = np_high_low(turn)
+    edge = ((0, wide - length), (0, wide - length))
+    cosine = jnp.asarray(np.pad(cosine, edge), F32)
+    sine = jnp.asarray(np.pad(sine, edge), F32)
+    sizes = (micro, coils, rows, length, parts)
+    slots = 2 * micro
+    return pl.pallas_call(
+        functools.partial(exchange_kernel, sizes),
+        out_shape=[
+            jax.ShapeDtypeStruct((slots, parts, 2 * rows, coils * rows), BF16),
+            jax.ShapeDtypeStruct((micro, 2 * wide, 2 * wide), BF16),
+            jax.ShapeDtypeStruct((micro, 2 * wide, 2 * wide), BF16),
+        ],
+        in_specs=[in_vmem()] * 8,
+        out_specs=[anywhere(), in_vmem(), in_vmem()],
+        scratch_shapes=[
+            pltpu.VMEM((slots, parts, 2 * rows, coils * rows), BF16),
+            pltpu.SemaphoreType.DMA((slots, parts - 1)),
+            pltpu.SemaphoreType.DMA((slots, parts - 1)),
+            pltpu.SemaphoreType.DMA((slots,)),
+        ],
+        compiler_params=params(collective_id=1, has_side_effects=True),
+        name="exchange",
+    )(kspace, maps, turn_high, turn_low, pick, mask, cosine, sine)
+
+
+def gather_lanes(blocks, coil, rows, wide):
+    pieces = [block[:, coil * rows : (coil + 1) * rows] for block in blocks]
+    height = pieces[0].shape[0]
+    short = wide - rows * len(pieces)
+    return jnp.concatenate(pieces + [jnp.zeros((height, short), pieces[0].dtype)], axis=1)
+
+
+def zero_fill_kernel(sizes, limit, fields, mask, fourier_high, fourier_low, filled, maps_out, edges):
+    coils, rows, length, parts = sizes
+    wide = padded(length)
+    chosen = mask[...].astype(BF16)
+    real = jnp.zeros((rows, wide), F32)
+    imag = jnp.zeros((rows, wide), F32)
+    group = 4
+    for first in range(0, coils, group):
+        stack = []
+        for coil in range(first, first + group):
+            on = jnp.where(coil < limit[pl.program_id(0)], 1.0, 0.0).astype(BF16)
+            maps_out[coil] = gather_lanes([fields[1, s] for s in range(parts)], coil, rows, wide) * on
+            stack.append(gather_lanes([fields[0, s] for s in range(parts)], coil, rows, wide) * chosen)
+        stack = jnp.concatenate(stack, axis=0)
+        turned = dot(stack, fourier_high[...]) + dot(stack, fourier_low[...])
+        for place in range(group):
+            top = 2 * rows * place
+            upper, lower = turned[top : top + rows], turned[top + rows : top + 2 * rows]
+            field_re = upper[:, :wide] - lower[:, wide:]
+            field_im = upper[:, wide:] + lower[:, :wide]
+            sense = maps_out[first + place].astype(F32)
+            sense_re, sense_im = sense[:rows], sense[rows:]
+            real = real + sense_re * field_re + sense_im * field_im
+            imag = imag + sense_re * field_im - sense_im * field_re
+    filled[0] = real
+    filled[1] = imag
+    put_edges(edges, real, imag)
+
+
+def put_edges(edges, real, imag):
+    rows, wide = real.shape
+    zeros = jnp.zeros((6, wide), F32)
+    edges[0] = jnp.concatenate([real[:1], imag[:1], zeros], axis=0)
+    edges[1] = jnp.concatenate([real[rows - 1 :], imag[rows - 1 :], zeros], axis=0)
+
+
+def zero_fill(fields, mask, limit, rows, length):
+    slots, parts, slabs, lanes = fields.shape
+    micro, coils, wide = slots // 2, lanes // rows, padded(length)
+    cosine, sine = phases(length)
+    table = np.zeros((wide, 2, wide))
+    table[:length, 0, :length] = cosine
+    table[:length, 1, :length] = sine
+    high, low = np_high_low(table.reshape(wide, 2 * wide))
+    sizes = (coils, rows, length, parts)
+    return pl.pallas_call(
+        functools.partial(zero_fill_kernel, sizes),
+        grid_spec=pltpu.PrefetchScalarGridSpec(
+            num_scalar_prefetch=1,
+            grid=(micro,),
+            in_specs=[
+                pl.BlockSpec((None, 2, parts, slabs, lanes), lambda b, _: (b, 0, 0, 0, 0)),
+                pl.BlockSpec((None, 1, wide), lambda b, _: (b, 0, 0)),
+                pl.BlockSpec((wide, 2 * wide), lambda b, _: (0, 0)),
+                pl.BlockSpec((wide, 2 * wide), lambda b, _: (0, 0)),
+            ],
+            out_specs=[
+                pl.BlockSpec((None, 2, rows, wide), lambda b, _: (b, 0, 0, 0)),
+                pl.BlockSpec((None, coils, slabs, wide), lambda b, _: (b, 0, 0, 0)),
+                pl.BlockSpec((2, None, 8, wide), lambda b, _: (0, b, 0, 0)),
+            ],
+        ),
+        out_shape=[
+            jax.ShapeDtypeStruct((micro, 2, rows, wide), F32),
+            jax.ShapeDtypeStruct((micro, coils, slabs, wide), BF16),
+            jax.ShapeDtypeStruct((2, micro, 8, wide), F32),
+        ],
+        compiler_params=params(),
+        name="zero_fill",
+    )(limit, fields.reshape(micro, 2, parts, slabs, lanes), mask, high, low)
+
+
+def start_halo(parts, sources, target, send, receive):
+    image, me = lax.axis_index("img"), lax.axis_index("row")
+    left, right = lax.rem(me + parts - 1, parts), lax.rem(me + 1, parts)
+    return [
+        remote(sources[0], target.at[1], send.at[0], receive.at[0], (image, left)),
+        remote(sources[1], target.at[0], send.at[1], receive.at[1], (image, right)),
+    ]
+
+
+def halo_kernel(parts, edges, halo, send, receive):
+    image, me = lax.axis_index("img"), lax.axis_index("row")
+    greet([(image, lax.rem(me + parts - 1, parts)), (image, lax.rem(me + 1, parts))])
+    for copy in start_halo(parts, (edges.at[0], edges.at[1]), halo, send, receive):
+        copy.wait()
+
+
+def halo_exchange(edges, parts, identity):
+    return pl.pallas_call(
+        functools.partial(halo_kernel, parts),
+        out_shape=jax.ShapeDtypeStruct(edges.shape, edges.dtype),
+        in_specs=[in_vmem()],
+        out_specs=in_vmem(),
+        scratch_shapes=[pltpu.SemaphoreType.DMA((2,)), pltpu.SemaphoreType.DMA((2,))],
+        compiler_params=params(collective_id=identity, has_side_effects=True),
+        name="halo",
+    )(edges)
+
+
+def sum_rows_kernel(parts, values, totals, held, send, receive):
+    peers = row_peers(parts)
+    greet(peers)
+    copies = [
+        remote(values, held.at[index], send.at[index], receive.at[index], peer)
+        for index, peer in enumerate(peers)
+    ]
+    total = values[...]
+    for index, copy in enumerate(copies):
+        copy.wait_recv()
+        total = total + held[index]
+    totals[...] = total
+    for copy in copies:
+        copy.wait_send()
+
+
+def sum_rows(values, parts, identity):
+    return pl.pallas_call(
+        functools.partial(sum_rows_kernel, parts),
+        out_shape=jax.ShapeDtypeStruct(values.shape, F32),
+        in_specs=[in_vmem()],
+        out_specs=in_vmem(),
+        scratch_shapes=[
+            pltpu.VMEM((parts - 1,) + values.shape, F32),
+            pltpu.SemaphoreType.DMA((parts - 1,)),
+            pltpu.SemaphoreType.DMA((parts - 1,)),
+        ],
+        compiler_params=params(collective_id=identity, has_side_effects=True),
+        name="sum_rows",
+    )(values)
+
+
+def lane_row(columns):
+    return jnp.sum(columns.T, axis=0, keepdims=True)
+
+
+def spread_row(row):
+    return jnp.broadcast_to(row, (TILE, TILE)).T
+
+
+def merge(sums, squares, count):
+    total = functools.reduce(jnp.add, sums)
+    mean = total / (count * len(sums))
+    square = None
+    for part, own in zip(sums, squares):
+        shift = part / count - mean
+        term = own + count * shift * shift
+        square = term if square is None else square + term
+    return total, square
+
+
+def layer_sums_kernel(
+    backward, parts, images, count, layer, stats, affine, extra, halo, coefs, rows_out, message, held, second, held_second, send, receive, send_halo, receive_halo
+):
+    image, me = lax.axis_index("img"), lax.axis_index("row")
+    rows, cols = row_peers(parts), image_peers(images)
+    greet(rows + cols)
+    width = layer.shape[1]
+    halos = start_halo(parts, (layer.at[:, 0], layer.at[:, width - 1]), halo, send_halo, receive_halo)
+    channels = stats.shape[0] * stats.shape[2]
+    first = lane_row(stats[:, 0].reshape(channels, TILE))
+    other = lane_row(stats[:, 1].reshape(channels, TILE))
+    message[...] = jnp.concatenate([first, other, extra[...], jnp.zeros((5, TILE), F32)], axis=0)
+
+    def exchange_step(source, peers, target, base):
+        copies = [
+            remote(source, target.at[index], send.at[base + index], receive.at[base + index], peer)
+            for index, peer in enumerate(peers)
+        ]
+        blocks = [source[...]]
+        for index, copy in enumerate(copies):
+            copy.wait_recv()
+            blocks.append(target[index])
+        return copies, blocks
+
+    def join(blocks, number):
+        added = functools.reduce(jnp.add, blocks)
+        if backward:
+            return added[0:1], added[1:2], added[2:3]
+        total, square = merge([b[0:1] for b in blocks], [b[1:2] for b in blocks], number)
+        return total, square, added[2:3]
+
+    sent, blocks = exchange_step(message, rows, held, 0)
+    first, other, plain = join(blocks, count)
+    second[...] = jnp.concatenate([first, other, plain, jnp.zeros((5, TILE), F32)], axis=0)
+    sent_second, blocks = exchange_step(second, cols, held_second, parts - 1)
+    first, other, plain = join(blocks, count * parts)
+    pixels = count * parts * images
+    if backward:
+        gain, inverse, offset = affine[0:1], affine[2:3], affine[3:4]
+        scale = inverse * gain
+        coefs[0] = spread_row(scale)
+        coefs[1] = spread_row(-scale * inverse * other / pixels)
+        coefs[2] = spread_row(-scale * (first + offset * other) / pixels)
+        rows_out[...] = jnp.concatenate([first, other, jnp.zeros((6, TILE), F32)], axis=0)
+    else:
+        gain, shift = affine[0:1], affine[1:2]
+        mean = first / pixels
+        inverse = lax.rsqrt(other / pixels + EPS_NORM)
+        offset = -mean * inverse
+        coefs[0] = spread_row(0.5 * gain * inverse)
+        coefs[1] = spread_row(0.5 * (shift + gain * offset))
+        coefs[2] = spread_row(inverse)
+        coefs[3] = spread_row(offset)
+        rows_out[...] = jnp.concatenate([gain, shift, inverse, offset, plain, jnp.zeros((3, TILE), F32)], axis=0)
+    for copy in sent + sent_second:
+        copy.wait_send()
+    for copy in halos:
+        copy.wait()
+
+
+def layer_sums(layer, stats, affine, extra, parts, images, count, backward, identity):
+    micro, width, channels, wide = layer.shape
+    number = 3 if backward else 4
+    return pl.pallas_call(
+        functools.partial(layer_sums_kernel, backward, parts, images, count),
+        out_shape=[
+            jax.ShapeDtypeStruct((2, micro, channels, wide), F32),
+            jax.ShapeDtypeStruct((number, TILE, TILE), F32),
+            jax.ShapeDtypeStruct((8, TILE), F32),
+        ],
+        in_specs=[anywhere(), in_vmem(), in_vmem(), in_vmem()],
+        out_specs=[anywhere(), in_vmem(), in_vmem()],
+        scratch_shapes=[
+            pltpu.VMEM((8, TILE), F32),
+            pltpu.VMEM((parts - 1, 8, TILE), F32),
+            pltpu.VMEM((8, TILE), F32),
+            pltpu.VMEM((images - 1, 8, TILE), F32),
+            pltpu.SemaphoreType.DMA((parts + images - 2,)),
+            pltpu.SemaphoreType.DMA((parts + images - 2,)),
+            pltpu.SemaphoreType.DMA((2,)),
+            pltpu.SemaphoreType.DMA((2,)),
+        ],
+        compiler_params=params(collective_id=identity, has_side_effects=True),
+        name="layer_sums_back" if backward else "layer_sums",
+    )(layer, stats, affine, extra)
+
+
+def repeat_lanes(block, wide):
+    return jnp.concatenate([block] * (wide // TILE), axis=1)
+
+
+def lane_mask(length, wide):
+    whole = length // TILE * TILE
+
+    def clear(values):
+        tail = values[:, whole:]
+        keep = lax.broadcasted_iota(jnp.int32, tail.shape, 1) < length - whole
+        return jnp.concatenate([values[:, :whole], jnp.where(keep, tail, 0.0)], axis=1)
+
+    return clear
+
+
+def fold(values):
+    parts = [values[:, at : at + TILE] for at in range(0, values.shape[1], TILE)]
+    return functools.reduce(jnp.add, parts)
+
+
+def put_shifted(stack, values, at):
+    channels, wide = values.shape
+    stack[0:channels, pl.ds(at, wide)] = pltpu.roll(values, 1, 1)
+    stack[channels : 2 * channels, pl.ds(at, wide)] = values
+    stack[2 * channels : 3 * channels, pl.ds(at, wide)] = pltpu.roll(values, wide - 1, 1)
+
+
+def lane_at(column, wide):
+    return pl.multiple_of(column * wide, TILE) if not isinstance(column, int) else column * wide
+
+
+def columns_at(stack, column, number, wide):
+    return stack[:, pl.ds(lane_at(column, wide), number * wide)]
+
+
+def ring_sum(table, stack, carry, first, out_rows, wide, emit):
+    pieces = []
+    for pair in range(BLOCK // 2):
+        product = dot(table[...], columns_at(stack, first + 2 * pair, 2, wide))
+        pieces += [product[:, :wide], product[:, wide:]]
+    older, newer = carry[0:out_rows], carry[out_rows : 2 * out_rows]
+    for place, piece in enumerate(pieces):
+        emit(place, older + piece[2 * out_rows : 3 * out_rows])
+        older = newer + piece[out_rows : 2 * out_rows]
+        newer = piece[0:out_rows]
+    carry[0:out_rows] = older
+    carry[out_rows : 2 * out_rows] = newer
+
+
+def ring_start(table, stack, carry, out_rows, wide):
+    product = dot(table[...], stack[:, 0 : 2 * wide])
+    carry[0:out_rows] = product[0:out_rows, :wide] + product[out_rows : 2 * out_rows, wide:]
+    carry[out_rows : 2 * out_rows] = product[0:out_rows, wide:]
+
+
+def edge_flags(parts):
+    me = lax.axis_index("row")
+    return me > 0, me < parts - 1
+
+
+def block_loop(width, body):
+    blocks = width // BLOCK
+
+    def step(index, carry):
+        body(index, False)
+        return carry
+
+    lax.fori_loop(0, blocks - 1, step, 0)
+    body(blocks - 1, True)
+
+
+def finish_stats(out, stats, total, clear, width, length):
+    channels, wide = total.shape
+    mean = jnp.sum(total[...], axis=1, keepdims=True) / (width * length)
+
+    def step(index, square):
+        for place in range(BLOCK):
+            shift = clear(out[index * BLOCK + place] - mean)
+            square = square + shift * shift
+        return square
+
+    square = lax.fori_loop(0, width // BLOCK, step, jnp.zeros((channels, wide), F32))
+    stats[0] = fold(total[...])
+    stats[1] = fold(square)
+
+
+def first_kernel(length, stack, table, out, stats, carry, total):
+    width, channels, wide = out.shape
+    clear = lane_mask(length, wide)
+    ring_start(table, stack, carry, channels, wide)
+    total[...] = jnp.zeros_like(total)
+
+    def body(block, last):
+        def emit(place, value):
+            out[block * BLOCK + place] = value
+            total[...] += clear(value)
+
+        ring_sum(table, stack, carry, block * BLOCK + 2, channels, wide, emit)
+
+    block_loop(width, body)
+    finish_stats(out, stats, total, clear, width, length)
+
+
+def first_layer(stack, table, width, length):
+    micro, depth, lanes = stack.shape
+    wide = padded(length)
+    channels = table.shape[0] // 3
+    return pl.pallas_call(
+        functools.partial(first_kernel, length),
+        grid=(micro,),
+        in_specs=[
+            pl.BlockSpec((None, depth, lanes), lambda b: (b, 0, 0)),
+            pl.BlockSpec(table.shape, lambda b: (0, 0)),
+        ],
+        out_specs=[
+            pl.BlockSpec((None, width, channels, wide), lambda b: (b, 0, 0, 0)),
+            pl.BlockSpec((None, 2, channels, TILE), lambda b: (b, 0, 0, 0)),
+        ],
+        out_shape=[
+            jax.ShapeDtypeStruct((micro, width, channels, wide), F32),
+            jax.ShapeDtypeStruct((micro, 2, channels, TILE), F32),
+        ],
+        scratch_shapes=[pltpu.VMEM((2 * channels, wide), F32), pltpu.VMEM((channels, wide), F32)],
+        compiler_params=params(),
+        name="first_layer",
+    )(stack, table)
+
+
+def silu_half(values, scale, offset):
+    half = values * scale + offset
+    curve = jnp.tanh(half)
+    return half, curve
+
+
+def middle_kernel(length, parts, last_layer, source, halo, coefs, table, *rest):
+    if last_layer:
+        out, stack, carry = rest
+    else:
+        out, stats, stack, carry, total = rest
+    width, channels, wide = source.shape
+    rows = table.shape[0] // 3
+    clear = lane_mask(length, wide)
+    scale, offset = repeat_lanes(coefs[0], wide), repeat_lanes(coefs[1], wide)
+    inner_left, inner_right = edge_flags(parts)
+
+    def put(values, column, keep=None):
+        half, curve = silu_half(values, scale, offset)
+        active = clear(half * curve + half)
+        if keep is not None:
+            active = jnp.where(keep, active, 0.0)
+        put_shifted(stack, active.astype(BF16), lane_at(column, wide))
+
+    put(halo[0], 0, inner_left)
+    put(source[0], 1)
+    ring_start(table, stack, carry, rows, wide)
+    if not last_layer:
+        total[...] = jnp.zeros_like(total)
+
+    def body(block, last):
+        for place in range(BLOCK):
+            column = block * BLOCK + 2 + place
+            if last and place == BLOCK - 1:
+                put(halo[1], column, inner_right)
+            else:
+                put(source[column - 1], column)
+
+        def emit(place, value):
+            out[block * BLOCK + place] = value
+            if not last_layer:
+                total[...] += clear(value)
+
+        ring_sum(table, stack, carry, block * BLOCK + 2, rows, wide, emit)
+
+    block_loop(width, body)
+    if not last_layer:
+        finish_stats(out, stats, total, clear, width, length)
+
+
+def layer_spec(width, channels, wide):
+    return pl.BlockSpec((None, width, channels, wide), lambda b: (b, 0, 0, 0))
+
+
+def halo_spec(channels, wide):
+    return pl.BlockSpec((2, None, channels, wide), lambda b: (0, b, 0, 0))
+
+
+def coef_spec(number, channels):
+    return pl.BlockSpec((number, channels, TILE), lambda b: (0, b, 0))
+
+
+def middle_layer(source, halo, coefs, table, length, parts, last_layer):
+    micro, width, channels, wide = source.shape
+    rows = table.shape[0] // 3
+    out_specs = [layer_spec(width, rows, wide)]
+    out_shape = [jax.ShapeDtypeStruct((micro, width, rows, wide), F32)]
+    scratch = [pltpu.VMEM((3 * channels, (width + 2) * wide), BF16), pltpu.VMEM((2 * rows, wide), F32)]
+    if not last_layer:
+        out_specs.append(pl.BlockSpec((None, 2, rows, TILE), lambda b: (b, 0, 0, 0)))
+        out_shape.append(jax.ShapeDtypeStruct((micro, 2, rows, TILE), F32))
+        scratch.append(pltpu.VMEM((rows, wide), F32))
+    return pl.pallas_call(
+        functools.partial(middle_kernel, length, parts, last_layer),
+        grid=(micro,),
+        in_specs=[
+            layer_spec(width, channels, wide),
+            halo_spec(channels, wide),
+            coef_spec(4, channels),
+            pl.BlockSpec(table.shape, lambda b: (0, 0)),
+        ],
+        out_specs=out_specs,
+        out_shape=out_shape,
+        scratch_shapes=scratch,
+        compiler_params=params(),
+        name="last_layer" if last_layer else "middle_layer",
+    )(source, halo, coefs, table)
+
+
+def backward_kernel(length, parts, given, *refs):
+    if given:
+        stack_in, below, below_halo, below_coefs, table, out, stats, weight_out, inputs, slope, carry, total, along = refs
+        stack = stack_in
+    else:
+        (
+            grads, grads_halo, layer, layer_halo, coefs, below, below_halo, below_coefs, table,
+            out, stats, weight_out, stack, inputs, slope, carry, total, along,
+        ) = refs
+    width, channels, wide = below.shape
+    clear = lane_mask(length, wide)
+    inner_left, inner_right = edge_flags(parts)
+    scale, offset = repeat_lanes(below_coefs[0], wide), repeat_lanes(below_coefs[1], wide)
+    if not given:
+        on_grad, on_layer, base = (repeat_lanes(coefs[index], wide) for index in range(3))
+
+    def put_grad(values, linear, column, keep=None):
+        upstream = clear(on_grad * values + on_layer * linear + base)
+        if keep is not None:
+            upstream = jnp.where(keep, upstream, 0.0)
+        put_shifted(stack, upstream.astype(BF16), lane_at(column, wide))
+
+    def put_input(values, column, keep=None):
+        half, curve = silu_half(values, scale, offset)
+        active = clear(half * curve + half)
+        if keep is not None:
+            active = jnp.where(keep, active, 0.0)
+        inputs[:, pl.ds(lane_at(column, wide), wide)] = active.astype(BF16)
+        return half, curve
+
+    def put_inner(column):
+        half, curve = put_input(below[column - 1], column)
+        slope[column - 1] = 0.5 * (1.0 + curve) * (1.0 + half * (1.0 - curve))
+        if not given:
+            put_grad(grads[column - 1], layer[column - 1], column)
+
+    put_input(below_halo[0], 0, inner_left)
+    if not given:
+        put_grad(grads_halo[0], layer_halo[0], 0, inner_left)
+    put_inner(1)
+    ring_start(table, stack, carry, channels, wide)
+    total[...] = jnp.zeros_like(total)
+    along[...] = jnp.zeros_like(along)
+
+    @pl.when(pl.program_id(0) == 0)
+    def _():
+        weight_out[...] = jnp.zeros_like(weight_out)
+
+    def body(block, last):
+        for place in range(BLOCK):
+            column = block * BLOCK + 2 + place
+            if last and place == BLOCK - 1:
+                put_input(below_halo[1], column, inner_right)
+                if not given:
+                    put_grad(grads_halo[1], layer_halo[1], column, inner_right)
+            else:
+                put_inner(column)
+        inverse, centre = repeat_lanes(below_coefs[2], wide), repeat_lanes(below_coefs[3], wide)
+
+        def emit(place, value):
+            column = block * BLOCK + place
+            shaped = clear(value * slope[column])
+            out[column] = shaped
+            total[...] += shaped
+            along[...] += shaped * (below[column] * inverse + centre)
+
+        ring_sum(table, stack, carry, block * BLOCK + 2, channels, wide, emit)
+        first = block * BLOCK
+        around = jnp.concatenate([columns_at(inputs, first + tap, BLOCK, wide) for tap in range(3)], axis=0)
+        weight_out[...] += dot_nt(columns_at(stack, first + 1, BLOCK, wide), around)
+
+    block_loop(width, body)
+    stats[0] = fold(total[...])
+    stats[1] = fold(along[...])
+
+
+def backward_layer(grad_parts, below, below_halo, below_coefs, table, length, parts):
+    micro, width, channels, wide = below.shape
+    given = len(grad_parts) == 1
+    depth = table.shape[1]
+    scratch = [
+        pltpu.VMEM((channels, (width + 2) * wide), BF16),
+        pltpu.VMEM((width, channels, wide), F32),
+        pltpu.VMEM((2 * channels, wide), F32),
+        pltpu.VMEM((channels, wide), F32),
+        pltpu.VMEM((channels, wide), F32),
+    ]
+    if given:
+        grad_specs = [pl.BlockSpec((None,) + grad_parts[0].shape[1:], lambda b: (b, 0, 0))]
+    else:
+        upper = grad_parts[0].shape[2]
+        grad_specs = [
+            layer_spec(width, upper, wide),
+            halo_spec(upper, wide),
+            layer_spec(width, upper, wide),
+            halo_spec(upper, wide),
+            coef_spec(3, upper),
+        ]
+        scratch = [pltpu.VMEM((3 * upper, (width + 2) * wide), BF16)] + scratch
+    return pl.pallas_call(
+        functools.partial(backward_kernel, length, parts, given),
+        grid=(micro,),
+        in_specs=grad_specs
+        + [
+            layer_spec(width, channels, wide),
+            halo_spec(channels, wide),
+            coef_spec(4, channels),
+            pl.BlockSpec(table.shape, lambda b: (0, 0)),
+        ],
+        out_specs=[
+            layer_spec(width, channels, wide),
+            pl.BlockSpec((None, 2, channels, TILE), lambda b: (b, 0, 0, 0)),
+            pl.BlockSpec((depth, 3 * channels), lambda b: (0, 0)),
+        ],
+        out_shape=[
+            jax.ShapeDtypeStruct((micro, width, channels, wide), F32),
+            jax.ShapeDtypeStruct((micro, 2, channels, TILE), F32),
+            jax.ShapeDtypeStruct((depth, 3 * channels), F32),
+        ],
+        scratch_shapes=scratch,
+        compiler_params=params(),
+        name="backward_last" if given else "backward_layer",
+    )(*grad_parts, below, below_halo, below_coefs, table)
+
+
+def backward_first_kernel(length, grads, layer, coefs, image, weight_out, stack):
+    width, channels, wide = grads.shape
+    clear = lane_mask(length, wide)
+    on_grad, on_layer, base = (repeat_lanes(coefs[index], wide) for index in range(3))
+
+    @pl.when(pl.program_id(0) == 0)
+    def _():
+        weight_out[...] = jnp.zeros_like(weight_out)
+
+    def body(block, last):
+        for place in range(BLOCK):
+            column = block * BLOCK + place
+            upstream = clear(on_grad * grads[column] + on_layer * layer[column] + base)
+            put_shifted(stack, upstream.astype(BF16), place * wide)
+        around = jnp.concatenate([columns_at(image, block * BLOCK + tap, BLOCK, wide) for tap in range(3)], axis=0)
+        weight_out[...] += dot_nt(stack[...], around)
+
+    block_loop(width, body)
+
+
+def backward_first(grads, layer, coefs, image, length):
+    micro, width, channels, wide = grads.shape
+    depth = image.shape[1]
+    return pl.pallas_call(
+        functools.partial(backward_first_kernel, length),
+        grid=(micro,),
+        in_specs=[
+            layer_spec(width, channels, wide),
+            layer_spec(width, channels, wide),
+            coef_spec(3, channels),
+            pl.BlockSpec((None,) + image.shape[1:], lambda b: (b, 0, 0)),
+        ],
+        out_specs=pl.BlockSpec((3 * channels, 3 * depth), lambda b: (0, 0)),
+        out_shape=jax.ShapeDtypeStruct((3 * channels, 3 * depth), F32),
+        scratch_shapes=[pltpu.VMEM((3 * channels, BLOCK * wide), BF16)],
+        compiler_params=params(),
+        name="backward_first",
+    )(grads, layer, coefs, image)
+
+
+def apply_normal(image, maps, normal_high, normal_low):
+    coils, slabs, wide = maps.shape
+    rows = slabs // 2
+    real, imag = image
+    stack = []
+    for coil in range(coils):
+        sense = maps[coil].astype(F32)
+        sense_re, sense_im = sense[:rows], sense[rows:]
+        stack.append(
+            jnp.concatenate(
+                [sense_re * real - sense_im * imag, sense_re * imag + sense_im * real], axis=1
+            )
+        )
+    stack = jnp.concatenate(stack, axis=0).astype(BF16)
+    out_re = jnp.zeros((rows, wide), F32)
+    out_im = jnp.zeros((rows, wide), F32)
+    turned = dot(stack, normal_high[...]) + dot(stack, normal_low[...])
+    for coil in range(coils):
+        sense = maps[coil].astype(F32)
+        sense_re, sense_im = sense[:rows], sense[rows:]
+        field = turned[coil * rows : (coil + 1) * rows]
+        field_re, field_im = field[:, :wide], field[:, wide:]
+        out_re = out_re + sense_re * field_re + sense_im * field_im
+        out_im = out_im + sense_re * field_im - sense_im * field_re
+    return out_re, out_im
+
+
+def pair(ref):
+    return ref[0], ref[1]
+
+
+def put_pair(ref, values):
+    ref[0] = values[0]
+    ref[1] = values[1]
+
+
+def blend(*terms):
+    return tuple(functools.reduce(jnp.add, [factor * image[part] for factor, image in terms]) for part in range(2))
+
+
+def inner_of(left, right):
+    product = left[0] * right[0] + left[1] * right[1]
+    return jnp.sum(jnp.sum(product, axis=1, keepdims=True), axis=0, keepdims=True)
+
+
+def put_sums(ref, values):
+    filler = [jnp.zeros((1, TILE), F32)] * (8 - len(values))
+    ref[...] = jnp.concatenate([jnp.broadcast_to(value, (1, TILE)) for value in values] + filler, axis=0)
+
+
+def scalar_at(ref, index):
+    return ref[index : index + 1, 0:1]
+
+
+def solve_one_kernel(length, consts, filled, result, maps, normal_high, normal_low, denoised, right, mapped, sums):
+    _, rows, wide = filled.shape
+    inside = lax.broadcasted_iota(jnp.int32, (rows, wide), 1) < length
+    penalty = consts[2]
+    images = []
+    for part in range(2):
+        value = jnp.where(inside, filled[part] + result[part] + consts[part], 0.0)
+        denoised[part] = value
+        images.append(filled[part] + penalty * value)
+    put_pair(right, images)
+    mapped_now = blend((1.0, apply_normal(images, maps, normal_high, normal_low)), (penalty, images))
+    put_pair(mapped, mapped_now)
+    put_sums(sums, [inner_of(images, images), inner_of(images, mapped_now)])
+
+
+def solve_two_kernel(consts, right, mapped, totals, maps, normal_high, normal_low, residue, through, sums):
+    penalty = consts[2]
+    stepsize = scalar_at(totals, 0) / scalar_at(totals, 1)
+    start, image = pair(right), pair(mapped)
+    left_over = blend((1.0, start), (-stepsize, image))
+    put_pair(residue, left_over)
+    mapped_now = blend((1.0, apply_normal(left_over, maps, normal_high, normal_low)), (penalty, left_over))
+    put_pair(through, mapped_now)
+    put_sums(
+        sums,
+        [
+            inner_of(left_over, left_over),
+            inner_of(left_over, mapped_now),
+            inner_of(left_over, image),
+            inner_of(start, mapped_now),
+        ],
+    )
+
+
+def step_scalars(totals_one, totals_two):
+    norm_0, curve_0 = scalar_at(totals_one, 0), scalar_at(totals_one, 1)
+    norm_1 = scalar_at(totals_two, 0)
+    factor = norm_1 / norm_0
+    curve_1 = (
+        scalar_at(totals_two, 1)
+        + factor * (scalar_at(totals_two, 2) + scalar_at(totals_two, 3))
+        + factor * factor * curve_0
+    )
+    return norm_0, curve_0, norm_1, curve_1, factor
+
+
+def solve_three_kernel(consts, right, mapped, residue, through, totals_one, totals_two, target, chosen, search, searched, slope, sums):
+    norm_0, curve_0, norm_1, curve_1, factor = step_scalars(totals_one, totals_two)
+    start, image = pair(right), pair(mapped)
+    direction = blend((1.0, pair(residue)), (factor, start))
+    image_1 = blend((1.0, pair(through)), (factor, image))
+    put_pair(search, direction)
+    put_pair(searched, image_1)
+    state = blend((norm_0 / curve_0, start), (norm_1 / curve_1, direction))
+    weight = chosen[...]
+    difference = [state[part] - target[part] for part in range(2)]
+    grad = [consts[3] * 2.0 * weight * difference[part] for part in range(2)]
+    put_pair(slope, grad)
+    masked = [weight * difference[part] for part in range(2)]
+    put_sums(
+        sums,
+        [
+            inner_of(grad, direction),
+            inner_of(grad, start),
+            inner_of(grad, image),
+            inner_of(image_1, start),
+            inner_of(image_1, image),
+            inner_of(direction, direction),
+            inner_of(masked, difference),
+        ],
+    )
+
+
+def solve_four_kernel(
+    consts, right, mapped, residue, denoised, search, searched, slope, totals_one, totals_two, totals_three, own_sums, maps, normal_high, normal_low, grad_out, edges, sums
+):
+    penalty = consts[2]
+    norm_0, curve_0, norm_1, curve_1, factor = step_scalars(totals_one, totals_two)
+    step_0, step_1 = norm_0 / curve_0, norm_1 / curve_1
+    start, image, left_over = pair(right), pair(mapped), pair(residue)
+    image_1, grad = pair(searched), pair(slope)
+    grad_search, grad_start, grad_image = (scalar_at(totals_three, index) for index in range(3))
+    cross_start, cross_image = scalar_at(totals_three, 3), scalar_at(totals_three, 4)
+    residue_image = scalar_at(totals_two, 2)
+    curve_grad_1 = -grad_search * norm_1 / (curve_1 * curve_1)
+    norm_grad_1 = grad_search / curve_1
+    search_grad = blend((step_1, grad), (2.0 * curve_grad_1, image_1))
+    factor_grad = step_1 * grad_start + 2.0 * curve_grad_1 * cross_start
+    joint = step_1 * grad_image + 2.0 * curve_grad_1 * cross_image
+    norm_total = norm_grad_1 + factor_grad / norm_0
+    residue_full = blend((1.0, search_grad), (2.0 * norm_total, left_over))
+    step_grad = grad_start - (joint + 2.0 * norm_total * residue_image)
+    curve_grad_0 = -step_grad * norm_0 / (curve_0 * curve_0)
+    mapped_grad = blend((-step_0, residue_full), (curve_grad_0, start))
+    through = apply_normal(mapped_grad, maps, normal_high, normal_low)
+    norm_grad_0 = -factor_grad * norm_1 / (norm_0 * norm_0) + step_grad / curve_0
+    right_grad = blend(
+        (1.0, residue_full),
+        (factor, search_grad),
+        (step_0, grad),
+        (curve_grad_0, image),
+        (1.0, through),
+        (penalty, mapped_grad),
+        (2.0 * norm_grad_0, start),
+    )
+    penalty_part = (
+        curve_grad_1 * scalar_at(own_sums, 5) + inner_of(mapped_grad, start) + inner_of(right_grad, pair(denoised))
+    )
+    grad_pair = [penalty * right_grad[part] for part in range(2)]
+    put_pair(grad_out, grad_pair)
+    put_edges(edges, *grad_pair)
+    offsets = [jnp.sum(jnp.sum(grad_pair[part], axis=1, keepdims=True), axis=0, keepdims=True) for part in range(2)]
+    put_sums(sums, [offsets[0], offsets[1], penalty_part, scalar_at(own_sums, 6)])
+
+
+def solve_call(kernel, name, consts, operands, outputs):
+    def spec(shape, lead):
+        block = tuple(None if axis == lead else size for axis, size in enumerate(shape))
+        return pl.BlockSpec(block, lambda b: tuple(b if axis == lead else 0 for axis in range(len(shape))))
+
+    micro = operands[0].shape[0]
+    return pl.pallas_call(
+        kernel,
+        grid=(micro,),
+        in_specs=[pl.BlockSpec(memory_space=pltpu.SMEM)] + [spec(operand.shape, 0) for operand in operands],
+        out_specs=[spec(shape, lead) for shape, lead in outputs],
+        out_shape=[jax.ShapeDtypeStruct(shape, F32) for shape, _ in outputs],
+        compiler_params=params(),
+        name=name,
+    )(consts, *operands)
+
+
+def shifted_image(image, halo, parts):
+    micro, channels, width, wide = image.shape
+    me = lax.axis_index("row")
+    left = jnp.where(me > 0, halo[0, :, :channels], 0.0)[:, :, None]
+    right = jnp.where(me < parts - 1, halo[1, :, :channels], 0.0)[:, :, None]
+    wider = jnp.concatenate([left, image, right], axis=2).astype(BF16)
+    stack = jnp.concatenate([jnp.roll(wider, 1, 3), wider, jnp.roll(wider, -1, 3)], axis=1)
+    stack = stack.reshape(micro, 3 * channels, (width + 2) * wide)
+    return jnp.pad(stack, ((0, 0), (0, 16 - 3 * channels), (0, 0)))
+
+
+def forward_table(weight):
+    _, outputs, inputs = weight.shape
+    return weight.reshape(3, 3, outputs, inputs).transpose(1, 2, 0, 3).reshape(3 * outputs, 3 * inputs)
+
+
+def backward_table(weight):
+    _, outputs, inputs = weight.shape
+    flipped = weight.reshape(3, 3, outputs, inputs)[::-1, ::-1]
+    return flipped.transpose(1, 3, 0, 2).reshape(3 * inputs, 3 * outputs)
+
+
+def weight_grad_of(sums, outputs, inputs):
+    return sums.reshape(3, outputs, 3, inputs)[::-1].transpose(0, 2, 1, 3).reshape(9, outputs, inputs)
+
+
+def to_bands(image):
+    micro, planes, rows, length = image.shape
+    swapped = lax.all_to_all(image, "row", split_axis=3, concat_axis=2, tiled=True)
+    return swapped.transpose(0, 1, 3, 2)
+
+
+def fast_local(arrays):
+    (
+        kspace, coil_maps, target, row_mask, foreground, anatomy, first_weight, middle_weight, last_weight, norm_gains, norm_shifts, extra_params,
+    ) = arrays
+    micro, _, coils, _, rows, length = kspace.shape
+    channels = first_weight.shape[1]
+    parts, images = lax.axis_size("row"), lax.axis_size("img")
+    wide = padded(length)
+    count = rows * length
+    edge = wide - length
+    mask = row_mask.astype(F32)
+    mask_wide = jnp.pad(mask, ((0, 0), (0, 0), (0, edge)))
+    limit = jnp.where(anatomy[:, 0] == 0, BRAIN_COILS, COILS).astype(jnp.int32)
+    fields, normal_high, normal_low = exchange(kspace[:, 0], coil_maps[:, 0], mask_wide, parts)
+    filled, maps, edges = zero_fill(fields, mask_wide, limit, rows, length)
+    planes = jnp.concatenate([target[:, 0], foreground.astype(F32)], axis=1)
+    planes = jnp.pad(to_bands(planes), ((0, 0), (0, 0), (0, 0), (0, edge)))
+
+    low = [first_weight.astype(BF16)] + [middle_weight[index].astype(BF16) for index in range(3)] + [last_weight.astype(BF16)]
+    gains = jnp.tile(norm_gains, (1, micro))
+    shifts = jnp.tile(norm_shifts, (1, micro))
+    pixel_part = jnp.broadcast_to(jnp.sum(foreground).astype(F32), (1, TILE))
+
+    halo = halo_exchange(edges, parts, 2)
+    image_stack = shifted_image(filled, halo, parts)
+    table = jnp.pad(forward_table(low[0]), ((0, 0), (0, 16 - 3 * low[0].shape[2])))
+    layer, stats = first_layer(image_stack, table, rows, length)
+    kept = []
+    for index in range(4):
+        affine = jnp.pad(jnp.stack([gains[index], shifts[index]]), ((0, 6), (0, 0)))
+        halo, coefs, rows_out = layer_sums(layer, stats, affine, pixel_part, parts, images, count, False, 3)
+        kept.append((layer, halo, coefs, rows_out))
+        if index < 3:
+            layer, stats = middle_layer(layer, halo, coefs, forward_table(low[index + 1]), length, parts, False)
+    last = jnp.pad(low[4], ((0, 0), (0, 8 - low[4].shape[1]), (0, 0)))
+    (result,) = middle_layer(layer, halo, coefs, forward_table(last), length, parts, True)
+    result = result[:, :, :2].transpose(0, 2, 1, 3)
+    pixel_total = kept[0][3][4, 0]
+
+    penalty = jnp.exp(extra_params[2])
+    consts = jnp.stack([extra_params[0], extra_params[1], penalty, 1.0 / pixel_total])
+    shape, sums_shape = filled.shape, (micro, 8, TILE)
+    image_out, sums_out = (shape, 0), (sums_shape, 0)
+    denoised, right, mapped, sums = solve_call(
+        functools.partial(solve_one_kernel, length), "solve_one", consts,
+        [filled, result, maps, normal_high, normal_low], [image_out, image_out, image_out, sums_out],
+    )
+    totals_one = sum_rows(sums, parts, 4)
+    residue, through, sums = solve_call(
+        solve_two_kernel, "solve_two", consts,
+        [right, mapped, totals_one, maps, normal_high, normal_low], [image_out, image_out, sums_out],
+    )
+    totals_two = sum_rows(sums, parts, 4)
+    search, searched, slope, own_sums = solve_call(
+        solve_three_kernel, "solve_three", consts,
+        [right, mapped, residue, through, totals_one, totals_two, planes[:, :2], planes[:, 2]],
+        [image_out, image_out, image_out, sums_out],
+    )
+    totals_three = sum_rows(own_sums, parts, 4)
+    grad, edges, scalars = solve_call(
+        solve_four_kernel, "solve_four", consts,
+        [right, mapped, residue, denoised, search, searched, slope, totals_one, totals_two, totals_three, own_sums, maps, normal_high, normal_low],
+        [image_out, ((2, micro, 8, wide), 1), sums_out],
+    )
+
+    halo = halo_exchange(edges, parts, 2)
+    grad_stack = shifted_image(grad, halo, parts)
+    weight_sums = [None] * 5
+    gain_rows, shift_rows = [None] * 4, [None] * 4
+    table = jnp.pad(backward_table(low[4]), ((0, 0), (0, 16 - 3 * low[4].shape[1])))
+    layer, halo, coefs, rows_out = kept[3]
+    grads, stats, weight_sums[4] = backward_layer([grad_stack], layer, halo, coefs, table, length, parts)
+    for index in (3, 2, 1, 0):
+        layer, halo, coefs, rows_out = kept[index]
+        grads_halo, coefs_back, totals = layer_sums(grads, stats, rows_out, pixel_part, parts, images, count, True, 5)
+        shift_rows[index] = jnp.sum(totals[0].reshape(micro, channels), 0)
+        gain_rows[index] = jnp.sum(totals[1].reshape(micro, channels), 0)
+        if index > 0:
+            below, below_halo, below_coefs, _ = kept[index - 1]
+            grads, stats, weight_sums[index] = backward_layer(
+                [grads, grads_halo, layer, halo, coefs_back], below, below_halo, below_coefs, backward_table(low[index]), length, parts
+            )
+        else:
+            centre = jnp.pad(image_stack[:, 2:4], ((0, 0), (0, 14), (0, 0)))
+            weight_sums[0] = backward_first(grads, layer, coefs_back, centre, length)
+    first_grad = weight_grad_of(weight_sums[0], channels, 16)[:, :, :2]
+    middle_grad = jnp.stack([weight_grad_of(weight_sums[index], channels, channels) for index in (1, 2, 3)])
+    last_grad = weight_grad_of(weight_sums[4][:6], 2, channels)
+    scalars = jnp.sum(scalars[:, :, 0], axis=0)
+    extra_grad = jnp.stack([scalars[0], scalars[1], penalty * scalars[2]])
+    first_grad, middle_grad, last_grad, extra_grad, loss = lax.psum(
+        (first_grad, middle_grad, last_grad, extra_grad, scalars[3]), ("img", "row")
+    )
+    return (first_grad, middle_grad, last_grad, jnp.stack(gain_rows), jnp.stack(shift_rows), extra_grad, loss), pixel_total
+
+
+def local(
+    kspace,
+    coil_maps,
+    target,
+    row_mask,
+    foreground,
+    anatomy,
+    first_weight,
+    middle_weight,
+    last_weight,
+    norm_gains,
+    norm_shifts,
+    extra_params,
+    first_mean,
+    first_square,
+    middle_mean,
+    middle_square,
+    last_mean,
+    last_square,
+    gains_mean,
+    gains_square,
+    shifts_mean,
+    shifts_square,
+    extra_mean,
+    extra_square,
+):
+    arrays = (
+        kspace, coil_maps, target, row_mask, foreground, anatomy, first_weight, middle_weight, last_weight, norm_gains, norm_shifts, extra_params,
+    )
+    gradients = fast_local if fits(kspace, first_weight, lax.axis_size("row")) else general_local
+    totals, pixel_total = gradients(arrays)
     params = (first_weight, middle_weight, last_weight, norm_gains, norm_shifts, extra_params)
     moments = (
         (first_mean, first_square),

time: 2410 us -> 601 us (0.25)
  matrix products: 803 us -> 0 us
  blocking collectives: 618 us -> 39.8 us
  local copies, waits for them, and re-layouts: 566 us -> 34.6 us
  Pallas kernels: 0 us -> 415 us
  starting transfers between devices: 182 us -> 6.54 us
  other arithmetic: 142 us -> 23.4 us
  between operations: 74.1 us -> 19.6 us
  waiting for transfers between devices: 5.02 us -> 57.8 us
    dot_general x288 -> x0, matrix products: 803 us -> none  [the longest x72 286 us: conv_backward(): jnp.einsum('oi,borw->birw', weight[tap_index], window, preferred_element_...]
    psum x18 -> x1, blocking collectives: 618 us -> 39.8 us  [fast_local(): lax.psum((first_grad, middle_grad, last_grad, extra_grad, scalars[3]), ('...]
    pallas_call x0 -> x29, Pallas kernels: none -> 415 us  [the longest x8 121 us: layer_sums(): pl.pallas_call(functools.partial(layer_sums_kernel, backward, parts, imag...]
    unnamed x688 -> x43, local copies, waits for them, and re-layouts: 254 us -> 5.16 us
    convert_element_type x28 -> x8, local copies, waits for them, and re-layouts: 152 us -> 0.97 us  [the longest x6 0.88 us: fast_local(): middle_weight[index].astype(BF16)]
    all_to_all x20 -> x1, starting transfers between devices: 104 us -> 6.33 us  [to_bands(): lax.all_to_all(image, 'row', split_axis=3, concat_axis=2, tiled=True)]
    ppermute x36 -> x0, starting transfers between devices: 78.6 us -> none  [the longest x18 53.9 us: with_halo(): lax.ppermute(tail, axis, [(i, (i + 1) % count) for i in range(ends)])]
    all_to_all x16 -> x3, local copies, waits for them, and re-layouts: 79.1 us -> 1.13 us  [to_bands(): lax.all_to_all(image, 'row', split_axis=3, concat_axis=2, tiled=True)]
  transfers between devices with their start and end apart: 57 -> 2, of which waited for: 3 -> 1; matrix products, arithmetic and copies ran while one was open for 35% -> 5% of each run, Pallas kernels for 0% -> 45%
where the time goes in v1:
time: 601 us; the launch traced here: 597 us
  Pallas kernels  415 us (69%)
  waiting for transfers between devices  57.8 us (10%)
  blocking collectives  39.8 us (7%)
  local copies, waits for them, and re-layouts  34.6 us (6%)
  other arithmetic  23.4 us (4%)
  between operations  19.6 us (3%)
  starting transfers between devices  6.54 us (1%)
    pallas_call x8, Pallas kernels, layer_sums(): pl.pallas_call(functools.partial(layer_sums_kernel, backward, parts, imag...  121 us
    pallas_call x1, Pallas kernels, exchange(): pl.pallas_call(functools.partial(exchange_kernel, sizes), out_shape=[jax....  81.5 us
    pallas_call x4, Pallas kernels, backward_layer(): pl.pallas_call(functools.partial(backward_kernel, length, parts, given),...  76.7 us
    psum x1, waiting for transfers between devices, fast_local(): lax.psum((first_grad, middle_grad, last_grad, extra_grad, scalars[3]), ('...  57.8 us
    pallas_call x4, Pallas kernels, middle_layer(): pl.pallas_call(functools.partial(middle_kernel, length, parts, last_layer...  51.1 us
    psum x1, blocking collectives, fast_local(): lax.psum((first_grad, middle_grad, last_grad, extra_grad, scalars[3]), ('...  39.8 us
    pallas_call x4, Pallas kernels, solve_call(): pl.pallas_call(kernel, grid=(micro,), in_specs=[pl.BlockSpec(memory_space...  23 us
    pallas_call x3, Pallas kernels, sum_rows(): pl.pallas_call(functools.partial(sum_rows_kernel, parts), out_shape=jax.S...  20.7 us
  transfers between devices with their start and end apart: 2, of which 1 were waited for; matrix products, arithmetic and copies ran while one was open for 5% of the time, Pallas kernels for 45%

profile of v1, /device:TPU:0, one launch (start us, length us, event | category | flops | bytes accessed | tf_op | source)
XLA Modules:
  0.0 597.0 jit_solution(10142519194496244845)
XLA Ops:
  7.2 1.7 fusion.33
  8.9 1.0 pad_maximum_fusion.1
  9.9 1.0 copy.153
  10.9 2.6 reshape.303
  13.5 6.3 %all-to-all-start = ((f32[8,1,9600]{2,1,0:T(1,128)}), f32[8,1,9600]{2,1,0:T(1,128)S(1)}, u32[]{:S(2)}, u32[]{:S(2)}) async-start(f32[8,1,9600]{2,1,0:T(1,128)} %reshape.303), calls=%async_computation | async-start | bytes 614400 | tf_op jit(solution)/shard_map/all_to_all | solution.py:1396
  22.2 81.5 %exchange.1 = (bf16[4,8,80,640]{3,2,1,0:T(8,128)(2,1)}, bf16[2,768,768]{2,1,0:T(8,128)(2,1)}, bf16[2,768,768]{2,1,0:T(8,128)(2,1)}) custom-call(f32[2,16,2,40,320]{4,3,2,1,0:T(8,128)} %bitcast.107, f32[2,16,2,40,320]{4,3,2,1,0:T(8,128)} %bitcast.108, bf16[2,640,320]{2,1,0:T(8,128)(2,1)} %constant.46.clone.turn_high, ...), custom_call_target="tpu_custom_call" | custom-call | tf_op jit(solution)/shard_map/exchange/pallas_call | solution.py:535
  103.8 8.4 %zero_fill.1 = (f32[2,2,40,384]{3,2,1,0:T(8,128)}, bf16[2,16,80,384]{3,2,1,0:T(8,128)(2,1)}, f32[2,2,8,384]{3,2,1,0:T(8,128)}) custom-call(s32[2]{0:T(128)} %fusion.17.limit, bf16[2,2,8,80,640]{4,3,2,1,0:T(8,128)(2,1)} %bitcast.111, f32[2,1,384]{2,1,0:T(1,128)} %pad.43.mask, bf16[384,768]{1,0:T(8,128)(2,1)} %constant.50.clone.fourier_high, ...), custom_call_target="tpu_custom_call" | custom-call | tf_op jit(solution)/shard_map/zero_fill/pallas_call | solution.py:607
  112.1 7.5 %halo.2 = f32[2,2,8,384]{3,2,1,0:T(8,128)} custom-call(f32[2,2,8,384]{3,2,1,0:T(8,128)} %get-tuple-element.87.edges), custom_call_target="tpu_custom_call" | custom-call | tf_op jit(solution)/shard_map/halo/pallas_call | solution.py:651
  120.5 1.0 maximum_convert_fusion
  126.9 0.8 rev.29
  127.7 0.8 reshape.252.refs_8_
  128.5 0.8 reshape.245.table
  129.3 0.8 rev.28
  130.1 0.8 reshape.251.refs_8_
  130.9 0.8 reshape.246.table
  131.7 0.8 rev.30
  132.5 0.8 reshape.253.refs_8_
  133.3 0.8 reshape.244.table
  134.4 2.0 fusion.32
  136.3 9.2 %first_layer.1 = (f32[2,40,64,384]{3,2,1,0:T(8,128)}, f32[2,2,64,128]{3,2,1,0:T(8,128)}) custom-call(bf16[2,16,16128]{2,1,0:T(8,128)(2,1)} %get-tuple-element.194.stack, bf16[192,16]{1,0:T(8,128)(2,1)} %pad.45.table), custom_call_target="tpu_custom_call" | custom-call | tf_op jit(solution)/shard_map/first_layer/pallas_call | solution.py:907
  146.6 16.6 %layer_sums.4 = (f32[2,2,64,384]{3,2,1,0:T(8,128)}, f32[4,128,128]{2,1,0:T(8,128)}, f32[8,128]{1,0:T(8,128)}) custom-call(f32[2,40,64,384]{3,2,1,0:T(8,128)} %get-tuple-element.89.layer.source.refs_5_, f32[2,2,64,128]{3,2,1,0:T(8,128)} %get-tuple-element.90.stats, f32[8,128]{1,0:T(8,128)} %select_maximum_fusion.3.affine, f32[1,128]{1,0:T(1,128)} %broadcast_in_dim.25.extra), custom_call_target="tpu_custom_call" | custom-call | tf_op jit(solution)/shard_map/layer_sums/pallas_call | solution.py:776
  163.3 1.2 slice.186
  165.8 13.7 %middle_layer.3 = (f32[2,40,64,384]{3,2,1,0:T(8,128)}, f32[2,2,64,128]{3,2,1,0:T(8,128)}) custom-call(f32[2,40,64,384]{3,2,1,0:T(8,128)} %get-tuple-element.89.layer.source.refs_5_, f32[2,2,64,384]{3,2,1,0:T(8,128)} %get-tuple-element.92.halo.refs_6_, f32[4,128,128]{2,1,0:T(8,128)} %get-tuple-element.93.coefs.refs_7_, bf16[192,192]{1,0:T(8,128)(2,1)} %reshape.244.table), custom_call_target="tpu_custom_call" | custom-call | tf_op jit(solution)/shard_map/middle_layer/pallas_call | solution.py:1000
  180.1 15.2 %layer_sums.5 = (f32[2,2,64,384]{3,2,1,0:T(8,128)}, f32[4,128,128]{2,1,0:T(8,128)}, f32[8,128]{1,0:T(8,128)}) custom-call(f32[2,40,64,384]{3,2,1,0:T(8,128)} %get-tuple-element.94.layer.source.refs_5_.refs_2_, f32[2,2,64,128]{3,2,1,0:T(8,128)} %get-tuple-element.95.stats, f32[8,128]{1,0:T(8,128)} %select_maximum_fusion.2.affine, f32[1,128]{1,0:T(1,128)} %broadcast_in_dim.25.extra), custom_call_target="tpu_custom_call" | custom-call | tf_op jit(solution)/shard_map/layer_sums/pallas_call | solution.py:776
  195.3 13.7 %middle_layer.4 = (f32[2,40,64,384]{3,2,1,0:T(8,128)}, f32[2,2,64,128]{3,2,1,0:T(8,128)}) custom-call(f32[2,40,64,384]{3,2,1,0:T(8,128)} %get-tuple-element.94.layer.source.refs_5_.refs_2_, f32[2,2,64,384]{3,2,1,0:T(8,128)} %get-tuple-element.96.halo.refs_6_.refs_3_, f32[4,128,128]{2,1,0:T(8,128)} %get-tuple-element.97.coefs.refs_7_, ...), custom_call_target="tpu_custom_call" | custom-call | tf_op jit(solution)/shard_map/middle_layer/pallas_call | solution.py:1000
  209.6 14.2 %layer_sums.6 = (f32[2,2,64,384]{3,2,1,0:T(8,128)}, f32[4,128,128]{2,1,0:T(8,128)}, f32[8,128]{1,0:T(8,128)}) custom-call(f32[2,40,64,384]{3,2,1,0:T(8,128)} %get-tuple-element.98.layer.source.refs_5_.refs_2_, f32[2,2,64,128]{3,2,1,0:T(8,128)} %get-tuple-element.99.stats, f32[8,128]{1,0:T(8,128)} %select_maximum_fusion.1.affine, f32[1,128]{1,0:T(1,128)} %broadcast_in_dim.25.extra), custom_call_target="tpu_custom_call" | custom-call | tf_op jit(solution)/shard_map/layer_sums/pallas_call | solution.py:776
  223.8 13.9 %middle_layer.5 = (f32[2,40,64,384]{3,2,1,0:T(8,128)}, f32[2,2,64,128]{3,2,1,0:T(8,128)}) custom-call(f32[2,40,64,384]{3,2,1,0:T(8,128)} %get-tuple-element.98.layer.source.refs_5_.refs_2_, f32[2,2,64,384]{3,2,1,0:T(8,128)} %get-tuple-element.100.halo.refs_6_.refs_3_, f32[4,128,128]{2,1,0:T(8,128)} %get-tuple-element.101.coefs.refs_7_, ...), custom_call_target="tpu_custom_call" | custom-call | tf_op jit(solution)/shard_map/middle_layer/pallas_call | solution.py:1000
  238.3 15.2 %layer_sums.7 = (f32[2,2,64,384]{3,2,1,0:T(8,128)}, f32[4,128,128]{2,1,0:T(8,128)}, f32[8,128]{1,0:T(8,128)}) custom-call(f32[2,40,64,384]{3,2,1,0:T(8,128)} %get-tuple-element.102.layer.source.refs_1_.refs_2_, f32[2,2,64,128]{3,2,1,0:T(8,128)} %get-tuple-element.103.stats, f32[8,128]{1,0:T(8,128)} %select_maximum_fusion.affine, f32[1,128]{1,0:T(1,128)} %broadcast_in_dim.25.extra), custom_call_target="tpu_custom_call" | custom-call | tf_op jit(solution)/shard_map/layer_sums/pallas_call | solution.py:776
  253.4 9.7 %last_layer.1 = f32[2,40,8,384]{3,2,1,0:T(8,128)} custom-call(f32[2,40,64,384]{3,2,1,0:T(8,128)} %get-tuple-element.102.layer.source.refs_1_.refs_2_, f32[2,2,64,384]{3,2,1,0:T(8,128)} %get-tuple-element.104.halo.refs_2_.refs_3_, f32[4,128,128]{2,1,0:T(8,128)} %get-tuple-element.105.coefs.refs_3_, bf16[24,192]{1,0:T(8,128)(2,1)} %reshape.248.table), custom_call_target="tpu_custom_call" | custom-call | tf_op jit(solution)/shard_map/last_layer/pallas_call | solution.py:1000
  263.2 1.3 slice.232
  265.7 6.6 %solve_one.1 = (f32[2,2,40,384]{3,2,1,0:T(8,128)}, f32[2,2,40,384]{3,2,1,0:T(8,128)}, f32[2,2,40,384]{3,2,1,0:T(8,128)}, f32[2,8,128]{2,1,0:T(8,128)}) custom-call(f32[4]{0:T(128)} %pad_maximum_fusion.8.consts, f32[2,2,40,384]{3,2,1,0:T(8,128)} %get-tuple-element.88.filled, f32[2,2,40,384]{3,2,1,0:T(8,128)} %bitcast.121, ...), custom_call_target="tpu_custom_call" | custom-call | tf_op jit(solution)/shard_map/solve_one/pallas_call | solution.py:1357
  272.4 6.9 %sum_rows.3.totals.totals_one = f32[2,8,128]{2,1,0:T(8,128)} custom-call(f32[2,8,128]{2,1,0:T(8,128)} %get-tuple-element.111.values), custom_call_target="tpu_custom_call" | custom-call | tf_op jit(solution)/shard_map/sum_rows/pallas_call | solution.py:679
  279.3 6.7 %solve_two.1 = (f32[2,2,40,384]{3,2,1,0:T(8,128)}, f32[2,2,40,384]{3,2,1,0:T(8,128)}, f32[2,8,128]{2,1,0:T(8,128)}) custom-call(f32[4]{0:T(128)} %pad_maximum_fusion.8.consts, f32[2,2,40,384]{3,2,1,0:T(8,128)} %get-tuple-element.109.right, f32[2,2,40,384]{3,2,1,0:T(8,128)} %get-tuple-element.110.mapped, f32[2,8,128]{2,1,0:T(8,128)} %sum_rows.3.totals.totals_one, ...), custom_call_target="tpu_custom_call" | custom-call | tf_op jit(solution)/shard_map/solve_two/pallas_call | solution.py:1357
  285.9 6.9 %sum_rows.4.totals_two = f32[2,8,128]{2,1,0:T(8,128)} custom-call(f32[2,8,128]{2,1,0:T(8,128)} %get-tuple-element.115.values), custom_call_target="tpu_custom_call" | custom-call | tf_op jit(solution)/shard_map/sum_rows/pallas_call | solution.py:679
  293.4 1.4 reduce.33
  294.7 1.7 reshape.304
  298.5 2.3 solve_three.1
  300.8 6.9 %sum_rows.5.totals_three = f32[2,8,128]{2,1,0:T(8,128)} custom-call(f32[2,8,128]{2,1,0:T(8,128)} %get-tuple-element.119.values.own_sums), custom_call_target="tpu_custom_call" | custom-call | tf_op jit(solution)/shard_map/sum_rows/pallas_call | solution.py:679
  307.7 7.3 %solve_four.1 = (f32[2,2,40,384]{3,2,1,0:T(8,128)}, f32[2,2,8,384]{3,2,1,0:T(8,128)}, f32[2,8,128]{2,1,0:T(8,128)}) custom-call(f32[4]{0:T(128)} %pad_maximum_fusion.8.consts, f32[2,2,40,384]{3,2,1,0:T(8,128)} %get-tuple-element.109.right, f32[2,2,40,384]{3,2,1,0:T(8,128)} %get-tuple-element.110.mapped, f32[2,2,40,384]{3,2,1,0:T(8,128)} %get-tuple-element.112.residue, ...), custom_call_target="tpu_custom_call" | custom-call | tf_op jit(solution)/shard_map/solve_four/pallas_call | solution.py:1357
  315.1 6.6 %halo.3 = f32[2,2,8,384]{3,2,1,0:T(8,128)} custom-call(f32[2,2,8,384]{3,2,1,0:T(8,128)} %get-tuple-element.120.edges), custom_call_target="tpu_custom_call" | custom-call | tf_op jit(solution)/shard_map/halo/pallas_call | solution.py:651
  322.5 1.0 maximum_convert_fusion.1
  323.7 0.8 slice_reduce_fusion
  326.1 1.5 fusion.7.refs_0_
  327.6 13.7 %backward_last.1 = (f32[2,40,64,384]{3,2,1,0:T(8,128)}, f32[2,2,64,128]{3,2,1,0:T(8,128)}, f32[16,192]{1,0:T(8,128)}) custom-call(bf16[2,16,16128]{2,1,0:T(8,128)(2,1)} %fusion.7.refs_0_, f32[2,40,64,384]{3,2,1,0:T(8,128)} %get-tuple-element.102.layer.source.refs_1_.refs_2_, f32[2,2,64,384]{3,2,1,0:T(8,128)} %get-tuple-element.104.halo.refs_2_.refs_3_, ...), custom_call_target="tpu_custom_call" | custom-call | tf_op jit(solution)/shard_map/backward_last/pallas_call | solution.py:1116
  342.1 15.4 %layer_sums_back.4 = (f32[2,2,64,384]{3,2,1,0:T(8,128)}, f32[3,128,128]{2,1,0:T(8,128)}, f32[8,128]{1,0:T(8,128)}) custom-call(f32[2,40,64,384]{3,2,1,0:T(8,128)} %get-tuple-element.122.layer.refs_0_, f32[2,2,64,128]{3,2,1,0:T(8,128)} %get-tuple-element.123.stats, f32[8,128]{1,0:T(8,128)} %get-tuple-element.124.affine, f32[1,128]{1,0:T(1,128)} %broadcast_in_dim.25.extra), custom_call_target="tpu_custom_call" | custom-call | tf_op jit(solution)/shard_map/layer_sums_back/pallas_call | solution.py:776
  357.5 0.8 slice_reduce_fusion.1
  358.5 20.9 %backward_layer.3 = (f32[2,40,64,384]{3,2,1,0:T(8,128)}, f32[2,2,64,128]{3,2,1,0:T(8,128)}, f32[192,192]{1,0:T(8,128)}) custom-call(f32[2,40,64,384]{3,2,1,0:T(8,128)} %get-tuple-element.122.layer.refs_0_, f32[2,2,64,384]{3,2,1,0:T(8,128)} %get-tuple-element.125.refs_1_, f32[2,40,64,384]{3,2,1,0:T(8,128)} %get-tuple-element.102.layer.source.refs_1_.refs_2_, ...), custom_call_target="tpu_custom_call" | custom-call | tf_op jit(solution)/shard_map/backward_layer/pallas_call | solution.py:1116
  379.4 1.1 reshape.258
  380.6 14.5 %layer_sums_back.5 = (f32[2,2,64,384]{3,2,1,0:T(8,128)}, f32[3,128,128]{2,1,0:T(8,128)}, f32[8,128]{1,0:T(8,128)}) custom-call(f32[2,40,64,384]{3,2,1,0:T(8,128)} %get-tuple-element.127.layer.refs_0_, f32[2,2,64,128]{3,2,1,0:T(8,128)} %get-tuple-element.128.stats, f32[8,128]{1,0:T(8,128)} %get-tuple-element.129.affine, f32[1,128]{1,0:T(1,128)} %broadcast_in_dim.25.extra), custom_call_target="tpu_custom_call" | custom-call | tf_op jit(solution)/shard_map/layer_sums_back/pallas_call | solution.py:776
  395.1 0.8 slice_reduce_fusion.2
  396.1 20.9 %backward_layer.4 = (f32[2,40,64,384]{3,2,1,0:T(8,128)}, f32[2,2,64,128]{3,2,1,0:T(8,128)}, f32[192,192]{1,0:T(8,128)}) custom-call(f32[2,40,64,384]{3,2,1,0:T(8,128)} %get-tuple-element.127.layer.refs_0_, f32[2,2,64,384]{3,2,1,0:T(8,128)} %get-tuple-element.130.refs_1_, f32[2,40,64,384]{3,2,1,0:T(8,128)} %get-tuple-element.98.layer.source.refs_5_.refs_2_, ...), custom_call_target="tpu_custom_call" | custom-call | tf_op jit(solution)/shard_map/backward_layer/pallas_call | solution.py:1116
  417.0 1.1 reshape.257
  418.2 14.7 %layer_sums_back.6 = (f32[2,2,64,384]{3,2,1,0:T(8,128)}, f32[3,128,128]{2,1,0:T(8,128)}, f32[8,128]{1,0:T(8,128)}) custom-call(f32[2,40,64,384]{3,2,1,0:T(8,128)} %get-tuple-element.132.layer.refs_0_, f32[2,2,64,128]{3,2,1,0:T(8,128)} %get-tuple-element.133.stats, f32[8,128]{1,0:T(8,128)} %get-tuple-element.134.affine, f32[1,128]{1,0:T(1,128)} %broadcast_in_dim.25.extra), custom_call_target="tpu_custom_call" | custom-call | tf_op jit(solution)/shard_map/layer_sums_back/pallas_call | solution.py:776
  433.0 0.8 slice_reduce_fusion.3
  434.0 21.2 %backward_layer.5 = (f32[2,40,64,384]{3,2,1,0:T(8,128)}, f32[2,2,64,128]{3,2,1,0:T(8,128)}, f32[192,192]{1,0:T(8,128)}) custom-call(f32[2,40,64,384]{3,2,1,0:T(8,128)} %get-tuple-element.132.layer.refs_0_, f32[2,2,64,384]{3,2,1,0:T(8,128)} %get-tuple-element.135.refs_1_, f32[2,40,64,384]{3,2,1,0:T(8,128)} %get-tuple-element.94.layer.source.refs_5_.refs_2_, ...), custom_call_target="tpu_custom_call" | custom-call | tf_op jit(solution)/shard_map/backward_layer/pallas_call | solution.py:1116
  455.1 1.1 reshape.256
  456.4 1.0 pad_maximum_fusion
  457.4 15.3 %layer_sums_back.7 = (f32[2,2,64,384]{3,2,1,0:T(8,128)}, f32[3,128,128]{2,1,0:T(8,128)}, f32[8,128]{1,0:T(8,128)}) custom-call(f32[2,40,64,384]{3,2,1,0:T(8,128)} %get-tuple-element.137.layer.grads, f32[2,2,64,128]{3,2,1,0:T(8,128)} %get-tuple-element.138.stats, f32[8,128]{1,0:T(8,128)} %get-tuple-element.91.affine, f32[1,128]{1,0:T(1,128)} %broadcast_in_dim.25.extra), custom_call_target="tpu_custom_call" | custom-call | tf_op jit(solution)/shard_map/layer_sums_back/pallas_call | solution.py:776
  472.8 9.7 %backward_first.1 = f32[192,48]{1,0:T(8,128)} custom-call(f32[2,40,64,384]{3,2,1,0:T(8,128)} %get-tuple-element.137.layer.grads, f32[2,40,64,384]{3,2,1,0:T(8,128)} %get-tuple-element.89.layer.source.refs_5_, f32[3,128,128]{2,1,0:T(8,128)} %get-tuple-element.139.coefs, bf16[2,16,16128]{2,1,0:T(8,128)(2,1)} %get-tuple-element.193.image), custom_call_target="tpu_custom_call" | custom-call | tf_op jit(solution)/shard_map/backward_first/pallas_call | solution.py:1165
  482.5 1.0 copy.163
  483.5 0.8 slice_reduce_fusion.4
  484.8 39.8 %all-reduce.12 = (f32[9,64,2]{1,2,0:T(2,128)S(1)}, f32[9,2,64]{2,1,0:T(2,128)S(1)}, f32[3]{0:T(128)S(1)}, f32[]{:T(128)}) all-reduce(f32[9,64,2]{1,2,0:T(2,128)S(1)} %slice.237, f32[9,2,64]{2,1,0:T(2,128)S(1)} %bitcast.134, f32[3]{0:T(128)S(1)} %pad_maximum_fusion.9, f32[]{:T(128)} %bitcast.56), channel_id=1, replica_groups=mesh['img'=4,'row'=8] {'img','row'}, use_global_device_ids=true, to_apply=%region_1.2 | all-reduce | flops 2308 | bytes 18464 | tf_op jit(solution)/shard_map/psum | solution.py:1490
  527.6 57.8 %all-reduce.15.cloned.1.call-done = f32[3,9,64,64]{3,2,1,0:T(8,128)} async-done(((f32[3,9,64,64]{3,2,1,0:T(8,128)}), f32[3,9,64,64]{3,2,1,0:T(8,128)}) %all-reduce.15.cloned.1.call-update) | async-done | bytes 442384 | tf_op jit(solution)/shard_map/psum | solution.py:1490
  585.4 3.3 fusion.23
  (156 shorter events, 21.3 us)
Async XLA Ops:
  7.2 12.8 %copy-start = (f32[3,9,64,64]{3,2,1,0:T(8,128)S(1)}, f32[3,9,64,64]{3,2,1,0:T(8,128)}, u32[]{:S(2)}) copy-start(f32[3,9,64,64]{3,2,1,0:T(8,128)} %param.38) | copy-start | bytes 1327108
  13.5 279.4 %all-to-all-start = ((f32[8,1,9600]{2,1,0:T(1,128)}), f32[8,1,9600]{2,1,0:T(1,128)S(1)}, u32[]{:S(2)}, u32[]{:S(2)}) async-start(f32[8,1,9600]{2,1,0:T(1,128)} %reshape.303), calls=%async_computation | async-start | bytes 614400 | tf_op jit(solution)/shard_map/all_to_all | solution.py:1396
  19.8 565.6 %all-reduce.15.cloned.1.call-start = ((), (), s32[]{:S(2)}) async-start(), calls=%async_computation.1 | async-start | bytes 1769472 | tf_op jit(solution)/shard_map/psum | solution.py:1490
  20.0 1.1 copy-start.19
  20.0 1.6 copy-start.11
  103.7 18.0 %copy-start.16 = (f32[3]{0:T(128)S(1)}, f32[3]{0:T(128)}, u32[]{:S(2)}) copy-start(f32[3]{0:T(128)} %param.42) | copy-start | bytes 40
  103.7 19.3 %copy-start.9 = (f32[4,64]{1,0:T(4,128)S(1)}, f32[4,64]{1,0:T(4,128)}, u32[]{:S(2)}) copy-start(f32[4,64]{1,0:T(4,128)} %param.40) | copy-start | bytes 3076
  103.7 19.7 %copy-start.10 = (f32[4,64]{1,0:T(4,128)S(1)}, f32[4,64]{1,0:T(4,128)}, u32[]{:S(2)}) copy-start(f32[4,64]{1,0:T(4,128)} %param.41) | copy-start | bytes 3076
  103.7 20.0 %copy-start.4 = (f32[9,2,64]{2,1,0:T(2,128)S(1)}, f32[9,2,64]{2,1,0:T(2,128)}, u32[]{:S(2)}) copy-start(f32[9,2,64]{2,1,0:T(2,128)} %param.39) | copy-start | bytes 13828
  103.7 20.0 %copy-start.3 = (f32[9,64,2]{1,2,0:T(2,128)S(1)}, f32[9,64,2]{1,2,0:T(2,128)}, u32[]{:S(2)}) copy-start(f32[9,64,2]{1,2,0:T(2,128)} %param.37) | copy-start | bytes 13828
  472.7 51.9 %copy-start.5 = (f32[9,64,2]{1,2,0:T(2,128)S(1)}, f32[9,64,2]{1,2,0:T(2,128)}, u32[]{:S(2)}) copy-start(f32[9,64,2]{1,2,0:T(2,128)} %param.43) | copy-start | bytes 13828
  472.7 51.9 %copy-start.6 = (f32[9,64,2]{1,2,0:T(2,128)S(1)}, f32[9,64,2]{1,2,0:T(2,128)}, u32[]{:S(2)}) copy-start(f32[9,64,2]{1,2,0:T(2,128)} %param.44) | copy-start | bytes 13828
  472.7 52.5 %copy-start.7 = (f32[9,2,64]{2,1,0:T(2,128)S(1)}, f32[9,2,64]{2,1,0:T(2,128)}, u32[]{:S(2)}) copy-start(f32[9,2,64]{2,1,0:T(2,128)} %param.47) | copy-start | bytes 13828
  472.7 52.5 %copy-start.8 = (f32[9,2,64]{2,1,0:T(2,128)S(1)}, f32[9,2,64]{2,1,0:T(2,128)}, u32[]{:S(2)}) copy-start(f32[9,2,64]{2,1,0:T(2,128)} %param.48) | copy-start | bytes 13828
  472.7 53.1 %copy-start.12 = (f32[4,64]{1,0:T(4,128)S(1)}, f32[4,64]{1,0:T(4,128)}, u32[]{:S(2)}) copy-start(f32[4,64]{1,0:T(4,128)} %param.49) | copy-start | bytes 3076
  472.8 53.1 %copy-start.13 = (f32[4,64]{1,0:T(4,128)S(1)}, f32[4,64]{1,0:T(4,128)}, u32[]{:S(2)}) copy-start(f32[4,64]{1,0:T(4,128)} %param.50) | copy-start | bytes 3076
  472.8 53.7 %copy-start.14 = (f32[4,64]{1,0:T(4,128)S(1)}, f32[4,64]{1,0:T(4,128)}, u32[]{:S(2)}) copy-start(f32[4,64]{1,0:T(4,128)} %param.51) | copy-start | bytes 3076
  472.8 53.7 %copy-start.15 = (f32[4,64]{1,0:T(4,128)S(1)}, f32[4,64]{1,0:T(4,128)}, u32[]{:S(2)}) copy-start(f32[4,64]{1,0:T(4,128)} %param.52) | copy-start | bytes 3076
  472.8 54.3 %copy-start.17 = (f32[3]{0:T(128)S(1)}, f32[3]{0:T(128)}, u32[]{:S(2)}) copy-start(f32[3]{0:T(128)} %param.53) | copy-start | bytes 40
  472.8 54.3 %copy-start.18 = (f32[3]{0:T(128)S(1)}, f32[3]{0:T(128)}, u32[]{:S(2)}) copy-start(f32[3]{0:T(128)} %param.54) | copy-start | bytes 40
  472.8 112.6 %copy-start.1 = (f32[3,9,64,64]{3,2,1,0:T(8,128)S(1)}, f32[3,9,64,64]{3,2,1,0:T(8,128)}, u32[]{:S(2)}) copy-start(f32[3,9,64,64]{3,2,1,0:T(8,128)} %param.45) | copy-start | bytes 1327108
  472.8 112.6 %copy-start.2 = (f32[3,9,64,64]{3,2,1,0:T(8,128)S(1)}, f32[3,9,64,64]{3,2,1,0:T(8,128)}, u32[]{:S(2)}) copy-start(f32[3,9,64,64]{3,2,1,0:T(8,128)} %param.46) | copy-start | bytes 1327108
Sparse Core Ops, SparseCore 0:
  457.5 127.8 all-reduce.14
